TPU v7x, 256 devices: a whole 4x4x8 slice. The times are simulated.
256 devices in a mesh: pulse: 32 (over z, y), range: 8 (over x, core).
Axes of the slice: x: 4, y: 4, z: 8, core: 2. Of those that a mesh axis runs over, the one named last changes fastest.
Arguments:
- returns_matched: float32 [2, 2048, 2048], P(None, 'pulse', 'range'), may hold values from -6 to 6
- center_wavecount: float32 [1], replicated, may hold values from 2 to 4
- scene_center_distance: float32 [1], replicated, may hold values from 4 to 16
- input_span_offset: int32 [2048, 16], replicated, may hold values from 0 to 128
- filter_choice_list: int32 [16], replicated, may hold values from 0 to 7
- filter_coefficients: float32 [8, 8, 128], replicated, may hold values from -2 to 2
Outputs:
- image: float32 [2, 2048, 2048], P(None, 'pulse', 'range')
All inputs are finite; a program needn't handle non-finite values.
Results may differ from a plain program's by a relative error of at most 0.0003.
Values sent between devices are 32-bit elements; how exact they have to be, the bound alone decides.
No kernel may reach another device: no remote copies, remote signals or barrier semaphores. Data moves between devices by JAX's collectives and lax.ppermute only.
A program may use at most 64 MiB of HBM per device.

v0:
```python
import functools
import math

import jax
import jax.numpy as jnp
import ml_dtypes
import numpy as np
from jax import lax
from jax.experimental import pallas as pl
from jax.experimental.pallas import tpu as pltpu
from jax.sharding import PartitionSpec as P

BLK = 128
TAPS = 8
NW = 8
N = 2048
ROWS = 256
FEW = 8
LANES = 128
STRETCH = (BLK - TAPS) // (NW - 1)


def halves(table):
    high = table.astype(np.float32).astype(ml_dtypes.bfloat16)
    low = (table - high.astype(np.float64)).astype(np.float32).astype(ml_dtypes.bfloat16)
    return high, low


@functools.lru_cache(maxsize=None)
def tables():
    steps = np.arange(ROWS)
    angle = 2.0 * math.pi / ROWS * (steps[:, None] * steps[None, :] % ROWS)
    cosine, sine = np.cos(angle), np.sin(angle)
    perm = steps % 8 * 32 + steps // 8
    found = {
        "plain": halves(np.concatenate([cosine, sine])),
        "range_in": halves(np.concatenate([cosine[:, perm], sine[:, perm]])),
        "range_out": halves(np.concatenate([cosine[perm], sine[perm]])),
    }
    lane = np.arange(LANES)
    part, mid, low = lane // 64, lane // 8 % 8, lane % 8
    for name, digit in (("mid", mid), ("low", low)):
        turn = 2.0 * math.pi / N * (steps[:, None] * digit[None, :])
        sign = np.where(part == 0, 1.0, -1.0)
        found["tw_" + name] = (
            np.cos(turn).astype(np.float32),
            (np.sin(turn) * sign[None, :]).astype(np.float32),
        )
        other = low if name == "mid" else mid
        same = other[:, None] == other[None, :]
        eighth = 2.0 * math.pi / FEW * (digit[:, None] * digit[None, :] % FEW)
        for way, orient in (("fwd", -1.0), ("inv", 1.0)):
            real, imag = np.cos(eighth), orient * np.sin(eighth)
            mixed = np.where(
                part[:, None] == part[None, :],
                real,
                np.where(part[:, None] < part[None, :], imag, -imag),
            )
            found[f"few_{name}_{way}"] = halves(np.where(same, mixed, 0.0))
    return found


def split(x):
    high = x.astype(jnp.bfloat16)
    low = (x - high.astype(jnp.float32)).astype(jnp.bfloat16)
    return high, low


def dot(left, right):
    return jnp.dot(left, right, preferred_element_type=jnp.float32)


def left_dot(high, low, x):
    x_high, x_low = split(x)
    both = dot(high, jnp.concatenate([x_high, x_low], axis=1))
    return both[:, :LANES] + both[:, LANES:] + dot(low, x_high)


def right_dot(x, high, low):
    x_high, x_low = split(x)
    return dot(x_high, high) + (dot(x_low, high) + dot(x_high, low))


def swapped(x):
    return pltpu.roll(x, LANES // 2, 1)


def sign_row(orient):
    lane = lax.broadcasted_iota(jnp.int32, (1, LANES), 1)
    return jnp.where(lane < LANES // 2, -orient, orient).astype(jnp.float32)


def rows_dft(high_ref, low_ref, x, orient):
    both = left_dot(high_ref[...], low_ref[...], x)
    return both[:ROWS] + swapped(both[ROWS:]) * sign_row(orient)


def forward(x, lh, ll, tc, ts, gh, gl):
    y = rows_dft(lh, ll, x, -1.0)
    z = y * tc[...] + swapped(y) * ts[...]
    return right_dot(z, gh[...], gl[...])


def inverse(x, lh, ll, tc, ts, gh, gl):
    y = right_dot(x, gh[...], gl[...])
    z = y * tc[...] - swapped(y) * ts[...]
    return rows_dft(lh, ll, z, 1.0)


def exchange(parts):
    group = lax.broadcasted_iota(jnp.int32, parts[0].shape, 1) // 8
    parts = list(parts)
    for bit in range(4):
        step = 1 << bit
        keep = group // step % 2 == 0
        for first in range(16):
            if first & step:
                continue
            a, b = parts[first], parts[first + step]
            parts[first] = jnp.where(keep, a, pltpu.roll(b, 8 * step, 1))
            parts[first + step] = jnp.where(keep, pltpu.roll(a, LANES - 8 * step, 1), b)
    return parts


def pack_kernel(x_ref, out_ref, held):
    for half in range(2):
        held[half] = x_ref[:, :, half * LANES : (half + 1) * LANES]
    parts = []
    for q in range(16):
        part, low = divmod(q, 8)
        parts.append(
            jnp.concatenate(
                [
                    held[half, part, pl.ds(low, 8, stride=8), :] for half in range(2)
                ],
                axis=0,
            )
        )
    for g, one in enumerate(exchange(parts)):
        for half in range(2):
            out_ref[half * 16 + g] = one[half * 8 : half * 8 + 8]


def unpack_kernel(x_ref, out_ref, held):
    parts = [jnp.concatenate([x_ref[g], x_ref[16 + g]], axis=0) for g in range(16)]
    for q, one in enumerate(exchange(parts)):
        part, low = divmod(q, 8)
        for half in range(2):
            held[half, part, pl.ds(low, 8, stride=8), :] = one[half * 8 : half * 8 + 8]
    for half in range(2):
        out_ref[:, :, half * LANES : (half + 1) * LANES] = held[half]


def azimuth_kernel(x_ref, lh, ll, tc, ts, gh, gl, out_ref):
    x = x_ref[...].reshape(ROWS, LANES)
    out_ref[...] = forward(x, lh, ll, tc, ts, gh, gl)


def azimuth_back_kernel(x_ref, lh, ll, tc, ts, gh, gl, out_ref):
    y = inverse(x_ref[...], lh, ll, tc, ts, gh, gl) * (1.0 / (N * N))
    out_ref[...] = y.reshape(32, 8, LANES)


def prepare_kernel(
    rank_ref, count_ref, distance_ref, choice_ref, shift_ref, coef_ref,
    cos_ref, sin_ref, high_ref, low_ref, lane_ref,
):
    lane = lax.broadcasted_iota(jnp.int32, (ROWS, LANES), 1)
    row = lax.broadcasted_iota(jnp.int32, (ROWS, LANES), 0)
    kx = rank_ref[0] + ROWS * (lane // 8 % 8)
    kr = row + ROWS * (lane % 8)
    fx = ((kx + N // 2) % N - N // 2).astype(jnp.float32) / N
    fr = ((kr + N // 2) % N - N // 2).astype(jnp.float32) / N
    turns = distance_ref[0] * jnp.sqrt((count_ref[0] + fr) ** 2 - 0.25 * fx**2)
    radians = (turns - jnp.round(turns)) * (2.0 * math.pi)
    cos_ref[...] = jnp.cos(radians)
    sin_ref[...] = jnp.sin(radians) * sign_row(1.0)
    few_lane = lax.broadcasted_iota(jnp.int32, (8, LANES), 1)
    few_row = lax.broadcasted_iota(jnp.int32, (8, LANES), 0)
    own = few_lane // 8 % 8 == few_row
    col = lax.broadcasted_iota(jnp.int32, (16, LANES), 0)
    col_lane = lax.broadcasted_iota(jnp.int32, (16, LANES), 1)
    starts = shift_ref[...].astype(jnp.float32).astype(jnp.bfloat16)
    for half in range(2):
        pick = (col == 2 * (col_lane % 8) + half).astype(jnp.float32).astype(jnp.bfloat16)
        spread = jnp.where(own, dot(starts, pick), 0.0)
        lane_ref[half : half + 1, :] = jnp.sum(spread, axis=0, keepdims=True).astype(jnp.int32)
        one = lax.broadcasted_iota(jnp.int32, (1, LANES), 1) % 8
        chosen = jnp.zeros((1, LANES), jnp.int32)
        for j in range(8):
            chosen = jnp.where(one == j, choice_ref[2 * j + half], chosen)
        lane_ref[2 + half : 3 + half, :] = chosen
    lane_ref[4:8, :] = jnp.zeros((4, LANES), jnp.int32)
    columns = jnp.transpose(coef_ref[...])
    inside = lax.broadcasted_iota(jnp.int32, (BLK, 2 * BLK), 0)
    window = lax.broadcasted_iota(jnp.int32, (BLK, 2 * BLK), 1)
    for d in range(NW):
        ahead = window - inside * (BLK + STRETCH * d) // BLK
        band = jnp.zeros((BLK, 2 * BLK), jnp.float32)
        for t in range(TAPS):
            band = jnp.where(ahead == t, columns[:, d * TAPS + t : d * TAPS + t + 1], band)
        high, low = split(band)
        high_ref[d * BLK : (d + 1) * BLK, :] = high
        low_ref[d * BLK : (d + 1) * BLK, :] = low


def stolt(turned, bh, bl, lane_ref):
    lane = lax.broadcasted_iota(jnp.int32, (1, LANES), 1)
    following = jnp.where(lane % 8 == 7, 0.0, pltpu.roll(turned, LANES - 1, 1))
    long = jnp.concatenate([turned, following], axis=0)
    highs, lows = [], []
    for half in range(2):
        based = long[half * BLK : half * BLK + 3 * BLK]
        starts = lane_ref[half : half + 1, :]
        for bit in reversed(range(8)):
            step = 1 << bit
            flagged = starts // step % 2 == 1
            length = 2 * BLK + (step if step >= 8 else 8 if step > 1 else 0)
            if step < 8:
                moved = pltpu.roll(based, based.shape[0] - step, 0)
            else:
                moved = jnp.concatenate([based[step:], based[:step]], axis=0)
            based = jnp.where(flagged, moved[:length], based[:length])
        high, low = split(based)
        highs.append(high)
        lows.append(low)
    high, low = jnp.concatenate(highs, axis=1), jnp.concatenate(lows, axis=1)
    chosen = jnp.concatenate([lane_ref[2:3, :], lane_ref[3:4, :]], axis=1)
    result = jnp.zeros((BLK, 2 * LANES), jnp.float32)
    for d in range(NW):
        own = pl.ds(d * BLK, BLK)
        one = dot(bh[own, :], high) + (dot(bh[own, :], low) + dot(bl[own, :], high))
        result = jnp.where(chosen == d, one, result)
    return jnp.concatenate([result[:, :LANES], result[:, LANES:]], axis=0)


def range_kernel(
    x_ref, lh, ll, tc, ts, gh, gl, cos_ref, sin_ref, bh, bl, lane_ref, kh, kl, hh, hl, out_ref
):
    lines = forward(x_ref[...], lh, ll, tc, ts, gh, gl)
    turned = lines * cos_ref[...] + swapped(lines) * sin_ref[...]
    focused = stolt(turned, bh, bl, lane_ref)
    out_ref[...] = inverse(focused, kh, kl, tc, ts, hh, hl)


VMEM = pl.BlockSpec(memory_space=pltpu.VMEM)
SMEM = pl.BlockSpec(memory_space=pltpu.SMEM)
HELD = [pltpu.VMEM((2, 2, 64, LANES), jnp.float32)]


def call(kernel, shapes, *args, scalars=0, flops=10**8, scratch=()):
    return pl.pallas_call(
        kernel,
        out_shape=shapes,
        in_specs=[SMEM] * scalars + [VMEM] * (len(args) - scalars),
        out_specs=jax.tree.map(lambda _: VMEM, shapes),
        scratch_shapes=scratch,
        compiler_params=pltpu.CompilerParams(vmem_limit_bytes=32 * 2**20),
        cost_estimate=pl.CostEstimate(flops=flops, bytes_accessed=2**20, transcendentals=0),
    )(*args)


def f32(*shape):
    return jax.ShapeDtypeStruct(shape, jnp.float32)


def local(returns, center, distance, starts, choices, coefficients):
    known = tables()
    rank = lax.axis_index("pulse") * 8 + lax.axis_index("range")
    own_starts = lax.dynamic_index_in_dim(starts.reshape(8, ROWS, 16), rank, 1, keepdims=False)
    cosine, sine, band_high, band_low, lane_rows = call(
        prepare_kernel,
        (
            f32(ROWS, LANES),
            f32(ROWS, LANES),
            jax.ShapeDtypeStruct((NW * BLK, 2 * BLK), jnp.bfloat16),
            jax.ShapeDtypeStruct((NW * BLK, 2 * BLK), jnp.bfloat16),
            jax.ShapeDtypeStruct((8, LANES), jnp.int32),
        ),
        rank.reshape(1).astype(jnp.int32), center, distance, choices,
        own_starts, coefficients.reshape(NW * TAPS, BLK),
        scalars=4,
    )
    x = call(pack_kernel, f32(32, 8, LANES), returns, scratch=HELD)
    x = lax.all_to_all(x, "pulse", 0, 0, tiled=True)
    x = call(
        azimuth_kernel, f32(ROWS, LANES), x,
        *known["plain"], *known["tw_mid"], *known["few_mid_fwd"],
    )
    x = lax.all_to_all(x.reshape(ROWS, 1, LANES), ("pulse", "range"), 0, 0, tiled=True)
    x = call(
        range_kernel, f32(ROWS, LANES), x.reshape(ROWS, LANES),
        *known["range_in"], *known["tw_low"], *known["few_low_fwd"],
        cosine, sine, band_high, band_low, lane_rows,
        *known["range_out"], *known["few_low_inv"],
    )
    x = lax.all_to_all(x.reshape(ROWS, 1, LANES), ("pulse", "range"), 0, 0, tiled=True)
    x = call(
        azimuth_back_kernel, f32(32, 8, LANES), x.reshape(ROWS, LANES),
        *known["plain"], *known["tw_mid"], *known["few_mid_inv"],
    )
    x = lax.all_to_all(x, "pulse", 0, 0, tiled=True)
    return call(unpack_kernel, f32(2, 64, 256), x, scratch=HELD)


def solution(mesh):
    placed = (P(None, "pulse", "range"), P(), P(), P(), P(), P())
    return jax.shard_map(
        local, mesh=mesh, in_specs=placed, out_specs=P(None, "pulse", "range"), check_vma=False
    )
```

profile of v0, /device:TPU:1, one launch (start us, length us, event | category | flops | bytes accessed | tf_op | source)
XLA Modules:
  0.0 82.5 jit_solution(16129456434672440846)
XLA Ops:
  0.0 1.0 %copy-done.19 = f32[2,64,256]{2,1,0:T(8,128)S(1)} copy-done((f32[2,64,256]{2,1,0:T(8,128)S(1)}, f32[2,64,256]{2,1,0:T(8,128)}, u32[]{:S(2)}) %copy-start.19) | copy-done | bytes 131096
  1.0 0.3 shard_map.226
  1.3 21.2 %all_to_all.20.x_ref = f32[32,8,128]{2,1,0:T(8,128)S(1)} all-to-all(f32[32,8,128]{2,1,0:T(8,128)S(1)} %shard_map.226), channel_id=1, replica_groups=mesh['pulse'=32,'range'=8] {'pulse'}, dimensions={0} | all-to-all | bytes 262144 | tf_op jit(solution)/shard_map/all_to_all | solution.py:285
  22.5 0.0 copy-start.3
  22.5 0.9 %copy-done.3 = f32[256,128]{1,0:T(8,128)S(1)} copy-done((f32[256,128]{1,0:T(8,128)S(1)}, f32[256,128]{1,0:T(8,128)}, u32[]{:S(2)}) %copy-start.3) | copy-done | bytes 131096
  23.4 0.8 copy-done.17
  24.2 0.8 copy-done.18
  25.0 1.3 %shard_map.227 = f32[256,128]{1,0:T(8,128)} custom-call(f32[32,8,128]{2,1,0:T(8,128)S(1)} %all_to_all.20.x_ref, bf16[512,256]{1,0:T(8,128)(2,1)S(1)} %copy-done.1, bf16[512,256]{1,0:T(8,128)(2,1)S(1)} %copy-done, f32[256,128]{1,0:T(8,128)S(1)} %copy-done.3, f32[256,128]{1,0:T(8,128)S(1)} %copy-done.2, bf16[128,128]{1,0:T(8,128)(2,1)S(1)} %copy-done.18, ...), custom_call_target="tpu_custom_call" | custom-call | flops 100000000 | bytes 1048576 | tf_op jit(solution)/shard_map/pallas_call | solution.py:252
  26.3 8.3 %all-to-all-start.1 = ((f32[256,1,128]{2,1,0:T(1,128)}), f32[256,1,128]{2,1,0:T(1,128)S(1)}, u32[]{:S(2)}, u32[]{:S(2)}) async-start(f32[256,1,128]{2,1,0:T(1,128)} %bitcast.1), calls=%async_computation.1 | async-start | bytes 262144 | tf_op jit(solution)/shard_map/all_to_all | solution.py:290
  35.9 0.0 copy-start.7
  36.0 0.0 copy-start.5
  36.0 0.0 copy-start.6
  36.0 0.1 constant_dynamic-slice_fusion
  36.1 0.1 copy.27
  36.2 0.8 copy-done.20
  37.0 2.7 %shard_map.228 = (f32[256,128]{1,0:T(8,128)S(1)}, f32[256,128]{1,0:T(8,128)S(1)}, bf16[1024,256]{1,0:T(8,128)(2,1)S(1)}, bf16[1024,256]{1,0:T(8,128)(2,1)S(1)}, s32[8,128]{1,0:T(8,128)S(1)}) custom-call(s32[1]{0:T(128)} %bitcast.3.rank_ref, f32[1]{0:T(128)S(6)} %copy.30.count_ref, f32[1]{0:T(128)S(6)} %copy.31.distance_ref, s32[16]{0:T(128)S(1)} %copy-done.21, ...), custom_call_target="tpu_custom_call" | custom-call | flops 100000000 | bytes 1048576 | tf_op jit(solution)/shard_map/pallas_call | solution.py:252
  39.7 7.8 %all-to-all-done.1 = f32[256,1,128]{2,1,0:T(1,128)S(1)} async-done(((f32[256,1,128]{2,1,0:T(1,128)}), f32[256,1,128]{2,1,0:T(1,128)S(1)}, u32[]{:S(2)}, u32[]{:S(2)}) %all-to-all-start.1) | async-done | bytes 131104 | tf_op jit(solution)/shard_map/all_to_all | solution.py:290
  47.6 2.1 %shard_map.229 = f32[256,128]{1,0:T(8,128)S(1)} custom-call(f32[256,128]{1,0:T(8,128)S(1)} %bitcast.15, bf16[512,256]{1,0:T(8,128)(2,1)S(1)} %copy-done.8, bf16[512,256]{1,0:T(8,128)(2,1)S(1)} %copy-done.7, f32[256,128]{1,0:T(8,128)S(1)} %copy-done.10, f32[256,128]{1,0:T(8,128)S(1)} %copy-done.9, bf16[128,128]{1,0:T(8,128)(2,1)S(1)} %copy-done.14, ...), custom_call_target="tpu_custom_call" | custom-call | flops 100000000 | bytes 1048576 | tf_op jit(solution)/shard_map/pallas_call | solution.py:252
  49.7 0.0 copy-start.15
  49.7 0.0 copy-start.16
  49.7 18.7 %all_to_all.21 = f32[256,1,128]{2,1,0:T(1,128)S(1)} all-to-all(f32[256,1,128]{2,1,0:T(1,128)S(1)} %bitcast.16), channel_id=1, replica_groups=mesh['pulse'=32,'range'=8] {'pulse','range'}, dimensions={0} | all-to-all | bytes 262144 | tf_op jit(solution)/shard_map/all_to_all | solution.py:297
  68.4 0.7 shard_map.230
  69.1 12.4 %all_to_all.22.x_ref = f32[32,8,128]{2,1,0:T(8,128)S(1)} all-to-all(f32[32,8,128]{2,1,0:T(8,128)S(1)} %shard_map.230), channel_id=1, replica_groups=mesh['pulse'=32,'range'=8] {'pulse'}, dimensions={0} | all-to-all | bytes 262144 | tf_op jit(solution)/shard_map/all_to_all | solution.py:302
  81.5 1.0 %shard_map.231 = f32[2,64,256]{2,1,0:T(8,128)} custom-call(f32[32,8,128]{2,1,0:T(8,128)S(1)} %all_to_all.22.x_ref), custom_call_target="tpu_custom_call" | custom-call | flops 100000000 | bytes 1048576 | tf_op jit(solution)/shard_map/pallas_call | solution.py:252
  (36 shorter events, 0.1 us)
Async XLA Ops:
  0.0 22.5 %copy-start.2 = (f32[256,128]{1,0:T(8,128)S(1)}, f32[256,128]{1,0:T(8,128)}, u32[]{:S(2)}) copy-start(f32[256,128]{1,0:T(8,128)} %constant.56.clone.ts) | copy-start | bytes 393220
  0.0 22.5 %copy-start = (bf16[512,256]{1,0:T(8,128)(2,1)S(1)}, bf16[512,256]{1,0:T(8,128)(2,1)}, u32[]{:S(2)}) copy-start(bf16[512,256]{1,0:T(8,128)(2,1)} %constant.54.clone.ll) | copy-start | bytes 786436
  0.0 22.5 %copy-start.1 = (bf16[512,256]{1,0:T(8,128)(2,1)S(1)}, bf16[512,256]{1,0:T(8,128)(2,1)}, u32[]{:S(2)}) copy-start(bf16[512,256]{1,0:T(8,128)(2,1)} %constant.53.clone.lh) | copy-start | bytes 786436
  0.0 1.0 %copy-start.19 = (f32[2,64,256]{2,1,0:T(8,128)S(1)}, f32[2,64,256]{2,1,0:T(8,128)}, u32[]{:S(2)}) copy-start(f32[2,64,256]{2,1,0:T(8,128)} %x_ref.1) | copy-start | bytes 393220
  22.5 0.9 %copy-start.3 = (f32[256,128]{1,0:T(8,128)S(1)}, f32[256,128]{1,0:T(8,128)}, u32[]{:S(2)}) copy-start(f32[256,128]{1,0:T(8,128)} %constant.55.clone.tc) | copy-start | bytes 393220
  23.4 0.8 copy-start.17
  24.2 0.8 copy-start.18
  24.9 11.0 %copy-start.22 = (s32[2048,16]{0,1:T(8,128)S(1)}, s32[2048,16]{0,1:T(8,128)}, u32[]{:S(2)}) copy-start(s32[2048,16]{0,1:T(8,128)} %param.27) | copy-start | bytes 393220
  24.9 22.5 %copy-start.9 = (f32[256,128]{1,0:T(8,128)S(1)}, f32[256,128]{1,0:T(8,128)}, u32[]{:S(2)}) copy-start(f32[256,128]{1,0:T(8,128)} %constant.62.clone.ts) | copy-start | bytes 393220
  25.0 22.5 %copy-start.10 = (f32[256,128]{1,0:T(8,128)S(1)}, f32[256,128]{1,0:T(8,128)}, u32[]{:S(2)}) copy-start(f32[256,128]{1,0:T(8,128)} %constant.61.clone.tc) | copy-start | bytes 393220
  25.0 22.5 %copy-start.13 = (bf16[128,128]{1,0:T(8,128)(2,1)S(1)}, bf16[128,128]{1,0:T(8,128)(2,1)}, u32[]{:S(2)}) copy-start(bf16[128,128]{1,0:T(8,128)(2,1)} %constant.64.clone.gl) | copy-start | bytes 98308
  25.0 22.5 %copy-start.14 = (bf16[128,128]{1,0:T(8,128)(2,1)S(1)}, bf16[128,128]{1,0:T(8,128)(2,1)}, u32[]{:S(2)}) copy-start(bf16[128,128]{1,0:T(8,128)(2,1)} %constant.63.clone.gh) | copy-start | bytes 98308
  26.3 21.2 %copy-start.8 = (bf16[512,256]{1,0:T(8,128)(2,1)S(1)}, bf16[512,256]{1,0:T(8,128)(2,1)}, u32[]{:S(2)}) copy-start(bf16[512,256]{1,0:T(8,128)(2,1)} %constant.59.clone.lh) | copy-start | bytes 786436
  26.3 21.2 %all-to-all-start.1 = ((f32[256,1,128]{2,1,0:T(1,128)}), f32[256,1,128]{2,1,0:T(1,128)S(1)}, u32[]{:S(2)}, u32[]{:S(2)}) async-start(f32[256,1,128]{2,1,0:T(1,128)} %bitcast.1), calls=%async_computation.1 | async-start | bytes 262144 | tf_op jit(solution)/shard_map/all_to_all | solution.py:290
  34.6 1.7 %copy-start.21 = (s32[16]{0:T(128)S(1)}, s32[16]{0:T(128)}, u32[]{:S(2)}) copy-start(s32[16]{0:T(128)} %choice_ref.1) | copy-start | bytes 196
  35.9 11.6 %copy-start.7 = (bf16[512,256]{1,0:T(8,128)(2,1)S(1)}, bf16[512,256]{1,0:T(8,128)(2,1)}, u32[]{:S(2)}) copy-start(bf16[512,256]{1,0:T(8,128)(2,1)} %constant.60.clone.ll) | copy-start | bytes 786436
  35.9 11.6 %copy-start.12 = (bf16[128,128]{1,0:T(8,128)(2,1)S(1)}, bf16[128,128]{1,0:T(8,128)(2,1)}, u32[]{:S(2)}) copy-start(bf16[128,128]{1,0:T(8,128)(2,1)} %constant.67.clone.hh) | copy-start | bytes 98308
  36.0 11.6 %copy-start.5 = (bf16[512,256]{1,0:T(8,128)(2,1)S(1)}, bf16[512,256]{1,0:T(8,128)(2,1)}, u32[]{:S(2)}) copy-start(bf16[512,256]{1,0:T(8,128)(2,1)} %constant.66.clone.kl) | copy-start | bytes 786436
  36.0 11.6 %copy-start.6 = (bf16[512,256]{1,0:T(8,128)(2,1)S(1)}, bf16[512,256]{1,0:T(8,128)(2,1)}, u32[]{:S(2)}) copy-start(bf16[512,256]{1,0:T(8,128)(2,1)} %constant.65.clone.kh) | copy-start | bytes 786436
  36.2 0.8 copy-start.20
  37.0 10.6 %copy-start.11 = (bf16[128,128]{1,0:T(8,128)(2,1)S(1)}, bf16[128,128]{1,0:T(8,128)(2,1)}, u32[]{:S(2)}) copy-start(bf16[128,128]{1,0:T(8,128)(2,1)} %constant.68.clone.hl) | copy-start | bytes 98308
  49.7 18.8 %copy-start.4 = (f32[256,128]{1,0:T(8,128)S(1)}, f32[256,128]{1,0:T(8,128)}, u32[]{:S(2)}) copy-start(f32[256,128]{1,0:T(8,128)} %constant.55.clone.tc) | copy-start | bytes 393220
  49.7 18.7 %copy-start.15 = (bf16[128,128]{1,0:T(8,128)(2,1)S(1)}, bf16[128,128]{1,0:T(8,128)(2,1)}, u32[]{:S(2)}) copy-start(bf16[128,128]{1,0:T(8,128)(2,1)} %constant.70.clone.gl) | copy-start | bytes 98308
  49.7 18.7 %copy-start.16 = (bf16[128,128]{1,0:T(8,128)(2,1)S(1)}, bf16[128,128]{1,0:T(8,128)(2,1)}, u32[]{:S(2)}) copy-start(bf16[128,128]{1,0:T(8,128)(2,1)} %constant.69.clone.gh) | copy-start | bytes 98308
where the time goes:
time: 82.9 us; the launch traced here: 82.5 us
  blocking collectives  52.3 us (63%)
  starting transfers between devices  8.26 us (10%)
  Pallas kernels  8.13 us (10%)
  waiting for transfers between devices  7.82 us (9%)
  local copies, waits for them, and re-layouts  4.49 us (5%)
  between operations  1.54 us (2%)
    all_to_all x2, blocking collectives, local(): x = lax.all_to_all(x, 'pulse', 0, 0, tiled=True)  33.6 us
    all_to_all x1, blocking collectives, local(): lax.all_to_all(x.reshape(ROWS, 1, LANES), ('pulse', 'range'), 0, 0, tiled...  18.7 us
    all_to_all x1, starting transfers between devices, local(): lax.all_to_all(x.reshape(ROWS, 1, LANES), ('pulse', 'range'), 0, 0, tiled...  8.26 us
    pallas_call x6, Pallas kernels, call(): pl.pallas_call(kernel, out_shape=shapes, in_specs=[SMEM] * scalars + [VME...  8.13 us
    all_to_all x1, waiting for transfers between devices, local(): lax.all_to_all(x.reshape(ROWS, 1, LANES), ('pulse', 'range'), 0, 0, tiled...  7.82 us
    unnamed x47, local copies, waits for them, and re-layouts  4.28 us
  transfers between devices with their start and end apart: 1, of which 1 were waited for; matrix products, arithmetic and copies ran while one was open for 0% of the time, Pallas kernels for 3%

commit v1 on v0

v1 whole, which is shorter than its diff:
```python
import math

import jax
import jax.numpy as jnp
import ml_dtypes
import numpy as np
from jax import lax
from jax.experimental import pallas as pl
from jax.experimental.pallas import tpu as pltpu
from jax.sharding import PartitionSpec as P

BLK = 128
TAPS = 8
NW = 8
N = 2048
ROWS = 256
QUARTER = 64
FEW = 8
LANES = 128
STRETCH = (BLK - TAPS) // (NW - 1)


def halves(table):
    high = table.astype(np.float32).astype(ml_dtypes.bfloat16)
    low = (table - high.astype(np.float64)).astype(np.float32).astype(ml_dtypes.bfloat16)
    return high, low


def tables():
    steps = np.arange(QUARTER)
    angle = 2.0 * math.pi / QUARTER * (steps[:, None] * steps[None, :] % QUARTER)
    high, low = halves(np.concatenate([np.cos(angle), np.sin(angle)]))
    lane = np.arange(LANES)
    part, mid, last = lane // 64, lane // 8 % 8, lane % 8
    eighth = 2.0 * math.pi / FEW * (mid[:, None] * last[None, :] % FEW)
    cosine, sine = np.cos(eighth), np.sin(eighth)
    step = part[None, :] - part[:, None]
    few = np.where(step == 0, cosine, np.where(step > 0, -sine, sine))
    few = np.where(last[:, None] == mid[None, :], few, 0.0)
    few_high, few_low = halves(np.concatenate([few, few.T], axis=1))
    matrices = np.concatenate([np.concatenate([high, high, low, low], axis=1), few_high, few_low])
    outer = 2.0 * math.pi / N * (np.arange(ROWS)[:, None] * mid[None, :])
    inner = np.concatenate([2.0 * math.pi / ROWS * steps * r for r in range(1, 4)])
    inner = np.broadcast_to(inner[:, None], (3 * QUARTER, LANES))
    sign = np.where(part == 0, 1.0, -1.0)[None, :]
    turns = [np.cos(outer), np.sin(outer) * sign, np.cos(inner), np.sin(inner) * sign]
    return matrices, np.concatenate(turns).astype(np.float32)


def split(x):
    high = x.astype(jnp.bfloat16)
    low = (x - high.astype(jnp.float32)).astype(jnp.bfloat16)
    return high, low


def dot(left, right):
    return jnp.dot(left, right, preferred_element_type=jnp.float32)


def swapped(x):
    return pltpu.roll(x, LANES // 2, 1)


def sign_row(orient):
    lane = lax.broadcasted_iota(jnp.int32, (1, LANES), 1)
    return jnp.where(lane < LANES // 2, -orient, orient).astype(jnp.float32)


def times_i(x, orient):
    return swapped(x) * sign_row(orient)


def turned_by(x, cosine, sine, orient):
    other = swapped(x) * sine
    return x * cosine + other if orient < 0 else x * cosine - other


def butterfly(y, orient):
    even, gap = y[0] + y[2], y[0] - y[2]
    odd, side = y[1] + y[3], times_i(y[1] - y[3], orient)
    return [even + odd, gap + side, even - odd, gap - side]


def quarter_dft(blocks, matrix_ref, orient):
    high, low = split(jnp.concatenate(blocks, axis=1))
    both = dot(matrix_ref[: 2 * QUARTER], jnp.concatenate([high, low, high, low], axis=0))
    found = []
    for r in range(4):
        across = slice(r * LANES, (r + 1) * LANES)
        found.append(both[:QUARTER, across] + times_i(both[QUARTER:, across], orient))
    return found


def quarter_turns(y, turn_ref, orient):
    found = [y[0]]
    for r in range(1, 4):
        cosine = turn_ref[pl.ds(2 * ROWS + (r - 1) * QUARTER, QUARTER)]
        sine = turn_ref[pl.ds(2 * ROWS + (r + 2) * QUARTER, QUARTER)]
        found.append(turned_by(y[r], cosine, sine, orient))
    return found


def few_dft(x, matrix_ref, way):
    high, low = split(x)
    across = pl.ds(way * LANES, LANES)
    table_high = matrix_ref[pl.ds(LANES, LANES), across]
    table_low = matrix_ref[pl.ds(2 * LANES, LANES), across]
    return dot(
        jnp.concatenate([high, low, high, low], axis=1),
        jnp.concatenate([table_high, table_high, table_low, table_low], axis=0),
    )


def forward(x_ref, matrix_ref, turn_ref):
    y = [x_ref[pl.ds(r, QUARTER, stride=4), :] for r in range(4)]
    y = quarter_turns(quarter_dft(y, matrix_ref, -1.0), turn_ref, -1.0)
    z = jnp.concatenate(butterfly(y, -1.0), axis=0)
    return few_dft(turned_by(z, turn_ref[:ROWS], turn_ref[ROWS : 2 * ROWS], -1.0), matrix_ref, 0)


def inverse(x, matrix_ref, turn_ref, out_ref, scale=1.0):
    z = turned_by(few_dft(x, matrix_ref, 1), turn_ref[:ROWS], turn_ref[ROWS : 2 * ROWS], 1.0)
    y = butterfly([z[q * QUARTER : (q + 1) * QUARTER] for q in range(4)], 1.0)
    y = quarter_dft(quarter_turns(y, turn_ref, 1.0), matrix_ref, 1.0)
    for r in range(4):
        out_ref[pl.ds(r, QUARTER, stride=4), :] = y[r] * scale


def exchange(parts):
    group = lax.broadcasted_iota(jnp.int32, parts[0].shape, 1) // 8
    parts = list(parts)
    for bit in range(4):
        step = 1 << bit
        keep = group // step % 2 == 0
        for first in range(16):
            if first & step:
                continue
            a, b = parts[first], parts[first + step]
            parts[first] = jnp.where(keep, a, pltpu.roll(b, 8 * step, 1))
            parts[first + step] = jnp.where(keep, pltpu.roll(a, LANES - 8 * step, 1), b)
    return parts


def first_kernel(out_ref):
    out_ref[...] = jnp.zeros_like(out_ref)


def pack_kernel(count_ref, distance_ref, x_ref, first_ref, choice_ref, out_ref, held):
    for half in range(2):
        held[half] = x_ref[:, :, half * LANES : (half + 1) * LANES]
        parts = [held[half, q // 8, pl.ds(q % 8, 8, stride=8), :] for q in range(16)]
        for g, one in enumerate(exchange(parts)):
            out_ref[half * 16 + g] = one


def unpack_kernel(x_ref, out_ref, held, sems):
    copies = []
    for half in range(2):
        for q, one in enumerate(exchange([x_ref[half * 16 + g] for g in range(16)])):
            held[half, q // 8, pl.ds(q % 8, 8, stride=8), :] = one
        copies.append(
            pltpu.make_async_copy(
                held.at[half], out_ref.at[:, :, pl.ds(half * LANES, LANES)], sems.at[half]
            )
        )
        copies[half].start()
    for copy in copies:
        copy.wait()


def azimuth_kernel(x_ref, matrix_ref, turn_ref, out_ref):
    out_ref[...] = forward(x_ref, matrix_ref, turn_ref)


def azimuth_back_kernel(x_ref, matrix_ref, turn_ref, out_ref):
    inverse(x_ref[...], matrix_ref, turn_ref, out_ref, 1.0 / (N * N))


def own_rank():
    return lax.axis_index("range") * 32 + lax.axis_index("pulse")


def polynomial(u, terms):
    total = jnp.full_like(u, terms[-1])
    for term in reversed(terms[:-1]):
        total = total * u + term
    return total


def turn_tables(turns):
    halves_count = jnp.round(2.0 * turns)
    rest = turns - 0.5 * halves_count
    odd = halves_count - 2.0 * jnp.floor(0.5 * halves_count)
    sign = 1.0 - 2.0 * odd
    turn = 2.0 * math.pi
    even_terms = [(-1) ** k * turn ** (2 * k) / math.factorial(2 * k) for k in range(8)]
    odd_terms = [(-1) ** k * turn ** (2 * k + 1) / math.factorial(2 * k + 1) for k in range(7)]
    square = rest * rest
    return sign * polynomial(square, even_terms), sign * rest * polynomial(square, odd_terms)


def both_parts(table):
    first = lax.broadcasted_iota(jnp.int32, (1, LANES), 1) < LANES // 2
    other = swapped(table)
    upper, lower = jnp.where(first, table, other), jnp.where(first, other, table)
    return jnp.concatenate([upper, lower], axis=0)


def half_rows(lane):
    row = lax.broadcasted_iota(jnp.int32, (BLK, LANES), 0)
    return row + jnp.where(lane >= LANES // 2, BLK, 0)


def phase_tables(rank, count, distance):
    lane = lax.broadcasted_iota(jnp.int32, (1, LANES), 1)
    kx = rank + ROWS * (lane // 8 % 8)
    kr = half_rows(lane) + ROWS * (lane % 8)
    fx = jnp.where(kx >= N // 2, kx - N, kx).astype(jnp.float32) * (1.0 / N)
    fr = jnp.where(kr >= N // 2, kr - N, kr).astype(jnp.float32) * (1.0 / N)
    cosine, sine = turn_tables(distance * jnp.sqrt((count + fr) ** 2 - 0.25 * fx**2))
    return both_parts(cosine), both_parts(sine) * sign_row(1.0)


def lane_rows(rank, starts_ref, choice_ref):
    lane = lax.broadcasted_iota(jnp.int32, (1, LANES), 1)
    row = lax.broadcasted_iota(jnp.int32, (16, LANES), 0)
    tile = rank // LANES * LANES
    own = lane == rank - tile
    spread = jnp.zeros((16, LANES), jnp.float32)
    for k in range(FEW):
        at = pl.multiple_of(tile + ROWS * k, LANES)
        some = starts_ref[:, pl.ds(at, LANES)].astype(jnp.float32)
        one = jnp.sum(jnp.where(own, some, 0.0), axis=1, keepdims=True)
        spread = jnp.where(lane // 8 % 8 == k, one, spread)
    starts, chosen = [], []
    for half in range(2):
        mine = jnp.where(row == 2 * (lane % 8) + half, spread, 0.0)
        starts.append(jnp.sum(mine, axis=0, keepdims=True).astype(jnp.int32))
        picked = jnp.zeros((1, LANES), jnp.float32)
        for j in range(FEW):
            at = 2 * j + half
            picked = jnp.where(lane % 8 == j, choice_ref[:1, at : at + 1], picked)
        chosen.append(picked.astype(jnp.int32))
    return starts, jnp.concatenate(chosen, axis=1)


def write_bands(coef_ref, high_ref, low_ref):
    coef = coef_ref[...]
    columns = jnp.transpose(jnp.concatenate([coef, coef], axis=0))
    lane = lax.broadcasted_iota(jnp.int32, (16, LANES), 1)
    row = lax.broadcasted_iota(jnp.int32, (16, LANES), 0)
    for d in range(NW):
        slope = BLK + STRETCH * d
        for g in range(BLK // 16):
            least = 16 * g * slope // BLK
            most = (16 * g + 15) * slope // BLK + TAPS - 1
            start = (row + 16 * g) * slope // BLK
            rows = pl.ds(d * BLK + 16 * g, 16)
            for tile in range(2):
                across = pl.ds(tile * LANES, LANES)
                if least >= (tile + 1) * LANES or most < tile * LANES:
                    high_ref[rows, across] = jnp.zeros((16, LANES), jnp.bfloat16)
                    low_ref[rows, across] = jnp.zeros((16, LANES), jnp.bfloat16)
                    continue
                ahead = lane + tile * LANES - start
                inside = (ahead >= 0) & (ahead < TAPS)
                at = jnp.where(inside, ahead, 0) + d * TAPS
                taken = jnp.take_along_axis(
                    columns[16 * g : 16 * g + 16], at, axis=1, mode="promise_in_bounds"
                )
                high, low = split(jnp.where(inside, taken, 0.0))
                high_ref[rows, across] = high
                low_ref[rows, across] = low


def stolt(turned, bh, bl, all_starts, chosen):
    lane = lax.broadcasted_iota(jnp.int32, (1, LANES), 1)
    following = jnp.where(lane % 8 == 7, 0.0, pltpu.roll(turned, LANES - 1, 1))
    long = jnp.concatenate([turned, following], axis=0)
    highs, lows = [], []
    for half in range(2):
        based = long[half * BLK : half * BLK + 3 * BLK]
        starts = all_starts[half]
        for bit in reversed(range(8)):
            step = 1 << bit
            flagged = starts // step % 2 == 1
            length = 2 * BLK + (step if step >= 8 else 8 if step > 1 else 0)
            if step < 8:
                moved = pltpu.roll(based, based.shape[0] - step, 0)
            else:
                moved = jnp.concatenate([based[step:], based[:step]], axis=0)
            based = jnp.where(flagged, moved[:length], based[:length])
        high, low = split(based)
        highs.append(high)
        lows.append(low)
    high, low = jnp.concatenate(highs, axis=1), jnp.concatenate(lows, axis=1)
    windows = jnp.concatenate([high, low, high], axis=0)
    result = jnp.zeros((BLK, 2 * LANES), jnp.float32)
    for d in range(NW):
        own = pl.ds(d * BLK, BLK)
        band = jnp.concatenate([bh[own, :], bh[own, :], bl[own, :]], axis=1)
        result = jnp.where(chosen == d, dot(band, windows), result)
    return jnp.concatenate([result[:, :LANES], result[:, LANES:]], axis=0)


def range_kernel(
    count_ref, distance_ref, x_ref, matrix_ref, turn_ref, choice_ref, starts_ref, coef_ref,
    out_ref, bh, bl,
):
    rank = own_rank()
    lines = forward(x_ref, matrix_ref, turn_ref)
    cosine, sine = phase_tables(rank, count_ref[0], distance_ref[0])
    turned = lines * cosine + swapped(lines) * sine
    write_bands(coef_ref, bh, bl)
    starts, chosen = lane_rows(rank, starts_ref, choice_ref)
    focused = stolt(turned, bh, bl, starts, chosen)
    inverse(focused, matrix_ref, turn_ref, out_ref)


VMEM = pl.BlockSpec(memory_space=pltpu.VMEM)
SMEM = pl.BlockSpec(memory_space=pltpu.SMEM)
HBM = pl.BlockSpec(memory_space=pltpu.HBM)
HELD = pltpu.VMEM((2, 2, 64, LANES), jnp.float32)


def call(kernel, shapes, *args, scalars=0, outs=VMEM, scratch=()):
    return pl.pallas_call(
        kernel,
        out_shape=shapes,
        in_specs=[SMEM] * scalars + [VMEM] * (len(args) - scalars),
        out_specs=jax.tree.map(lambda _: outs, shapes),
        scratch_shapes=scratch,
        compiler_params=pltpu.CompilerParams(vmem_limit_bytes=32 * 2**20),
        cost_estimate=pl.CostEstimate(flops=10**10, bytes_accessed=2**20, transcendentals=0),
    )(*args)


def f32(*shape):
    return jax.ShapeDtypeStruct(shape, jnp.float32)


def bf16(*shape):
    return jax.ShapeDtypeStruct(shape, jnp.bfloat16)


def local(returns, center, distance, starts, choices, coefficients):
    whole = ("range", "pulse")
    known = tables()
    choices = choices.astype(jnp.float32).reshape(1, 16)
    first = call(first_kernel, f32(8, LANES))
    x = call(
        pack_kernel, f32(32, 8, LANES), center, distance, returns, first, choices,
        scalars=2, scratch=[HELD],
    )
    x = lax.all_to_all(x, "pulse", 0, 0, tiled=True)
    x = call(azimuth_kernel, f32(ROWS, LANES), x.reshape(ROWS, LANES), *known)
    x = lax.all_to_all(x.reshape(ROWS, 1, LANES), whole, 0, 0, tiled=True)
    x = call(
        range_kernel, f32(ROWS, LANES), center, distance, x.reshape(ROWS, LANES), *known,
        choices, starts.T, coefficients.reshape(NW * TAPS, BLK),
        scalars=2,
        scratch=[pltpu.VMEM((NW * BLK, 2 * BLK), jnp.bfloat16)] * 2,
    )
    x = lax.all_to_all(x.reshape(ROWS, 1, LANES), whole, 0, 0, tiled=True)
    x = call(azimuth_back_kernel, f32(ROWS, LANES), x.reshape(ROWS, LANES), *known)
    x = lax.all_to_all(x.reshape(32, 8, LANES), "pulse", 0, 0, tiled=True)
    return call(
        unpack_kernel, f32(2, 64, 256), x, outs=HBM,
        scratch=[HELD, pltpu.SemaphoreType.DMA((2,))],
    )


def solution(mesh):
    placed = (P(None, "pulse", "range"), P(), P(), P(), P(), P())
    return jax.shard_map(
        local, mesh=mesh, in_specs=placed, out_specs=P(None, "pulse", "range"), check_vma=False
    )
```

time: 82.9 us -> 80.1 us (0.966)
  blocking collectives: 52.3 us -> 73 us
  starting transfers between devices: 8.26 us -> 0 us
  waiting for transfers between devices: 7.82 us -> 0 us
  local copies, waits for them, and re-layouts: 4.49 us -> 0.04 us
  Pallas kernels: 8.13 us -> 5.29 us
    all_to_all x1 -> x3, blocking collectives: 18.7 us -> 51.7 us  [the longest x2 38.9 us: local(): x = lax.all_to_all(x.reshape(ROWS, 1, LANES), whole, 0, 0, tiled=True)]
    all_to_all x2 -> x1, blocking collectives: 33.6 us -> 21.3 us  [local(): x = lax.all_to_all(x, 'pulse', 0, 0, tiled=True)]
    all_to_all x1 -> x0, starting transfers between devices: 8.26 us -> none  [local(): lax.all_to_all(x.reshape(ROWS, 1, LANES), ('pulse', 'range'), 0, 0, tiled...]
    all_to_all x1 -> x0, waiting for transfers between devices: 7.82 us -> none  [local(): lax.all_to_all(x.reshape(ROWS, 1, LANES), ('pulse', 'range'), 0, 0, tiled...]
    unnamed x47 -> x12, local copies, waits for them, and re-layouts: 4.28 us -> 0.04 us
    pallas_call x6, Pallas kernels: 8.13 us -> 5.29 us  [call(): pl.pallas_call(kernel, out_shape=shapes, in_specs=[SMEM] * scalars + [VME...]
  transfers between devices with their start and end apart: 1 -> 0, of which waited for: 1 -> 0; matrix products, arithmetic and copies ran while one was open for 0% -> 0% of each run, Pallas kernels for 3% -> 0%
where the time goes in v1:
time: 80.1 us; the launch traced here: 79.8 us
  blocking collectives  73 us (91%)
  Pallas kernels  5.29 us (7%)
  between operations  1.44 us (2%)
    all_to_all x2, blocking collectives, local(): x = lax.all_to_all(x.reshape(ROWS, 1, LANES), whole, 0, 0, tiled=True)  38.9 us
    all_to_all x1, blocking collectives, local(): x = lax.all_to_all(x, 'pulse', 0, 0, tiled=True)  21.3 us
    all_to_all x1, blocking collectives, local(): x = lax.all_to_all(x.reshape(32, 8, LANES), 'pulse', 0, 0, tiled=True)  12.8 us
    pallas_call x6, Pallas kernels, call(): pl.pallas_call(kernel, out_shape=shapes, in_specs=[SMEM] * scalars + [VME...  5.29 us

profile of v1, /device:TPU:1, one launch (start us, length us, event | category | flops | bytes accessed | tf_op | source)
XLA Modules:
  0.0 79.8 jit_solution(496781631422344205)
XLA Ops:
  0.0 0.0 copy-start
  0.7 0.0 copy-start.5
  1.4 0.0 copy-done.5
  1.4 0.0 copy-done
  1.4 0.0 copy-start.3
  1.4 0.3 shard_map.83
  1.7 0.0 copy-start.4
  1.8 21.3 %all_to_all.20 = f32[32,8,128]{2,1,0:T(8,128)S(1)} all-to-all(f32[32,8,128]{2,1,0:T(8,128)S(1)} %shard_map.83), channel_id=1, replica_groups=mesh['pulse'=32,'range'=8] {'pulse'}, dimensions={0} | all-to-all | bytes 262144 | tf_op jit(solution)/shard_map/all_to_all | solution.py:355
  23.1 0.0 copy-done.3
  23.1 0.0 copy-done.4
  23.1 0.6 shard_map.84
  23.7 0.0 copy-start.1
  23.7 0.0 copy-start.2
  23.7 20.7 %all_to_all.21 = f32[256,1,128]{2,1,0:T(1,128)S(1)} all-to-all(f32[256,1,128]{2,1,0:T(1,128)S(1)} %bitcast.19), channel_id=1, replica_groups=mesh['pulse'=32,'range'=8] {'range','pulse'}, dimensions={0} | all-to-all | bytes 262144 | tf_op jit(solution)/shard_map/all_to_all | solution.py:357
  44.4 0.0 copy-done.1
  44.4 0.0 copy-done.2
  44.4 2.7 %shard_map.85 = f32[256,128]{1,0:T(8,128)S(1)} custom-call(f32[1]{0:T(128)S(6)} %copy.11.count_ref, f32[1]{0:T(128)S(6)} %copy.12.distance_ref, f32[256,128]{1,0:T(8,128)S(1)} %bitcast.14, bf16[384,256]{1,0:T(8,128)(2,1)S(1)} %copy-done.4, f32[896,128]{1,0:T(8,128)S(1)} %copy-done.3, f32[1,16]{1,0:T(1,128)S(1)} %convert_bitcast_fusion.choice_ref, ...), custom_call_target="tpu_custom_call" | custom-call | flops 10000000000 | bytes 1048576 | tf_op jit(solution)/shard_map/pallas_call | solution.py:327
  47.1 18.3 %all_to_all.22 = f32[256,1,128]{2,1,0:T(1,128)S(1)} all-to-all(f32[256,1,128]{2,1,0:T(1,128)S(1)} %bitcast.15), channel_id=1, replica_groups=mesh['pulse'=32,'range'=8] {'range','pulse'}, dimensions={0} | all-to-all | bytes 262144 | tf_op jit(solution)/shard_map/all_to_all | solution.py:364
  65.4 0.7 shard_map.86
  66.1 12.8 %all_to_all.23.x_ref = f32[32,8,128]{2,1,0:T(8,128)S(1)} all-to-all(f32[32,8,128]{2,1,0:T(8,128)S(1)} %bitcast.17), channel_id=1, replica_groups=mesh['pulse'=32,'range'=8] {'pulse'}, dimensions={0} | all-to-all | bytes 262144 | tf_op jit(solution)/shard_map/all_to_all | solution.py:366
  78.8 1.0 %shard_map.87 = f32[2,64,256]{2,1,0:T(8,128)} custom-call(f32[32,8,128]{2,1,0:T(8,128)S(1)} %all_to_all.23.x_ref), custom_call_target="tpu_custom_call" | custom-call | flops 10000000000 | bytes 1048576 | tf_op jit(solution)/shard_map/pallas_call | solution.py:327
  (2 shorter events, 0.0 us)
Async XLA Ops:
  0.0 1.4 %copy-start = (f32[2,64,256]{2,1,0:T(8,128)S(1)}, f32[2,64,256]{2,1,0:T(8,128)}, u32[]{:S(2)}) copy-start(f32[2,64,256]{2,1,0:T(8,128)} %x_ref.1) | copy-start | bytes 393220
  0.7 0.7 copy-start.5
  1.4 21.7 %copy-start.3 = (f32[896,128]{1,0:T(8,128)S(1)}, f32[896,128]{1,0:T(8,128)}, u32[]{:S(2)}) copy-start(f32[896,128]{1,0:T(8,128)} %constant.5.clone.turn_ref) | copy-start | bytes 1376260
  1.7 21.3 %copy-start.4 = (bf16[384,256]{1,0:T(8,128)(2,1)S(1)}, bf16[384,256]{1,0:T(8,128)(2,1)}, u32[]{:S(2)}) copy-start(bf16[384,256]{1,0:T(8,128)(2,1)} %constant.4.clone.matrix_ref) | copy-start | bytes 589828
  23.7 20.7 %copy-start.1 = (s32[2048,16]{0,1:T(8,128)S(1)}, s32[2048,16]{0,1:T(8,128)}, u32[]{:S(2)}) copy-start(s32[2048,16]{0,1:T(8,128)} %param.11) | copy-start | bytes 393220
  23.7 20.7 %copy-start.2 = (f32[8,8,128]{2,1,0:T(8,128)S(1)}, f32[8,8,128]{2,1,0:T(8,128)}, u32[]{:S(2)}) copy-start(f32[8,8,128]{2,1,0:T(8,128)} %param.13) | copy-start | bytes 98308

commit v2 on v1

--- a/solution.py
+++ b/solution.py
@@ -26,24 +26,36 @@
     return high, low
 
 
+FIRST, LAST = slice(0, 128), slice(128, 192)
+INTO, INTO_I, BACK, BACK_I = (slice(at, at + 128) for at in range(192, 704, 128))
+
+
 def tables():
     steps = np.arange(QUARTER)
     angle = 2.0 * math.pi / QUARTER * (steps[:, None] * steps[None, :] % QUARTER)
-    high, low = halves(np.concatenate([np.cos(angle), np.sin(angle)]))
+    cosine, sine = np.cos(angle), np.sin(angle)
+    high, low = halves(np.concatenate([cosine, -sine]))
+    first = np.concatenate([high, high, low, low], axis=1)
+    last = np.concatenate(halves(np.concatenate([cosine, sine], axis=1)), axis=1)
     lane = np.arange(LANES)
-    part, mid, last = lane // 64, lane // 8 % 8, lane % 8
-    eighth = 2.0 * math.pi / FEW * (mid[:, None] * last[None, :] % FEW)
+    part, mid, low_digit = lane // 64, lane // 8 % 8, lane % 8
+    eighth = 2.0 * math.pi / FEW * (mid[:, None] * low_digit[None, :] % FEW)
     cosine, sine = np.cos(eighth), np.sin(eighth)
     step = part[None, :] - part[:, None]
     few = np.where(step == 0, cosine, np.where(step > 0, -sine, sine))
-    few = np.where(last[:, None] == mid[None, :], few, 0.0)
-    few_high, few_low = halves(np.concatenate([few, few.T], axis=1))
-    matrices = np.concatenate([np.concatenate([high, high, low, low], axis=1), few_high, few_low])
+    few = np.where(low_digit[:, None] == mid[None, :], few, 0.0)
+    times_i = np.where(lane[:, None] % 64 == lane[None, :] % 64, step, 0).astype(np.float64)
+    parts = []
+    for one in (few, few @ times_i, few.T, few.T @ times_i):
+        large = np.where(np.abs(one) > 0.9, np.round(one), 0.0)
+        small = np.where(large == 0, np.sign(np.round(2 * one)), 0.0)
+        parts.append(np.concatenate([large, small], axis=1))
+    whole = [part.astype(ml_dtypes.bfloat16) for part in parts]
+    matrices = np.concatenate([first, last, *whole])
     outer = 2.0 * math.pi / N * (np.arange(ROWS)[:, None] * mid[None, :])
     inner = np.concatenate([2.0 * math.pi / ROWS * steps * r for r in range(1, 4)])
     inner = np.broadcast_to(inner[:, None], (3 * QUARTER, LANES))
-    sign = np.where(part == 0, 1.0, -1.0)[None, :]
-    turns = [np.cos(outer), np.sin(outer) * sign, np.cos(inner), np.sin(inner) * sign]
+    turns = [np.cos(outer), np.sin(outer), np.cos(inner), np.sin(inner)]
     return matrices, np.concatenate(turns).astype(np.float32)
 
 
@@ -61,83 +73,90 @@
     return pltpu.roll(x, LANES // 2, 1)
 
 
-def sign_row(orient):
-    lane = lax.broadcasted_iota(jnp.int32, (1, LANES), 1)
-    return jnp.where(lane < LANES // 2, -orient, orient).astype(jnp.float32)
-
-
-def times_i(x, orient):
-    return swapped(x) * sign_row(orient)
-
-
-def turned_by(x, cosine, sine, orient):
-    other = swapped(x) * sine
-    return x * cosine + other if orient < 0 else x * cosine - other
-
-
-def butterfly(y, orient):
-    even, gap = y[0] + y[2], y[0] - y[2]
-    odd, side = y[1] + y[3], times_i(y[1] - y[3], orient)
-    return [even + odd, gap + side, even - odd, gap - side]
-
-
-def quarter_dft(blocks, matrix_ref, orient):
-    high, low = split(jnp.concatenate(blocks, axis=1))
-    both = dot(matrix_ref[: 2 * QUARTER], jnp.concatenate([high, low, high, low], axis=0))
-    found = []
-    for r in range(4):
-        across = slice(r * LANES, (r + 1) * LANES)
-        found.append(both[:QUARTER, across] + times_i(both[QUARTER:, across], orient))
-    return found
-
-
-def quarter_turns(y, turn_ref, orient):
+def turned_by(pair, cosine, sine):
+    a, b = pair
+    return a * cosine + b * sine, b * cosine - a * sine
+
+
+def butterfly(y):
+    (a0, b0), (a1, b1), (a2, b2), (a3, b3) = y
+    even, gap = (a0 + a2, b0 + b2), (a0 - a2, b0 - b2)
+    odd, side = (a1 + a3, b1 + b3), (b1 - b3, a3 - a1)
+    return [
+        (even[0] + odd[0], even[1] + odd[1]),
+        (gap[0] + side[0], gap[1] + side[1]),
+        (even[0] - odd[0], even[1] - odd[1]),
+        (gap[0] - side[0], gap[1] - side[1]),
+    ]
+
+
+def quarter_turns(y, turn_ref):
     found = [y[0]]
     for r in range(1, 4):
         cosine = turn_ref[pl.ds(2 * ROWS + (r - 1) * QUARTER, QUARTER)]
         sine = turn_ref[pl.ds(2 * ROWS + (r + 2) * QUARTER, QUARTER)]
-        found.append(turned_by(y[r], cosine, sine, orient))
+        found.append(turned_by(y[r], cosine, sine))
     return found
 
 
-def few_dft(x, matrix_ref, way):
+def few_dft(x, table):
+    both = dot(jnp.concatenate(x, axis=1), jnp.concatenate(table, axis=0))
+    return both[:, :LANES] + both[:, LANES:] * math.sqrt(0.5)
+
+
+def forward(x_ref, matrix_ref, turn_ref, sides=False):
+    x = jnp.concatenate([x_ref[pl.ds(r, QUARTER, stride=4), :] for r in range(4)], axis=1)
     high, low = split(x)
-    across = pl.ds(way * LANES, LANES)
-    table_high = matrix_ref[pl.ds(LANES, LANES), across]
-    table_low = matrix_ref[pl.ds(2 * LANES, LANES), across]
-    return dot(
-        jnp.concatenate([high, low, high, low], axis=1),
-        jnp.concatenate([table_high, table_high, table_low, table_low], axis=0),
-    )
-
-
-def forward(x_ref, matrix_ref, turn_ref):
-    y = [x_ref[pl.ds(r, QUARTER, stride=4), :] for r in range(4)]
-    y = quarter_turns(quarter_dft(y, matrix_ref, -1.0), turn_ref, -1.0)
-    z = jnp.concatenate(butterfly(y, -1.0), axis=0)
-    return few_dft(turned_by(z, turn_ref[:ROWS], turn_ref[ROWS : 2 * ROWS], -1.0), matrix_ref, 0)
+    both = dot(matrix_ref[FIRST], jnp.concatenate([high, low, high, low], axis=0))
+    y = []
+    for r in range(4):
+        one = both[:, r * LANES : (r + 1) * LANES]
+        y.append((one[:QUARTER], one[QUARTER:]))
+    y = butterfly(quarter_turns(y, turn_ref))
+    pair = [jnp.concatenate([one[at] for one in y], axis=0) for at in range(2)]
+    a, b = turned_by(pair, turn_ref[:ROWS], turn_ref[ROWS : 2 * ROWS])
+    into, into_i = matrix_ref[INTO], matrix_ref[INTO_I]
+    if not sides:
+        return few_dft([*split(a), *split(b)], [into, into, into_i, into_i])
+    lane = lax.broadcasted_iota(jnp.int32, (1, LANES), 1)
+    pieces = split(a + swapped(b * jnp.where(lane < LANES // 2, 1.0, -1.0)))
+    return few_dft(pieces, [into, into]), few_dft(pieces, [into_i, into_i])
 
 
 def inverse(x, matrix_ref, turn_ref, out_ref, scale=1.0):
-    z = turned_by(few_dft(x, matrix_ref, 1), turn_ref[:ROWS], turn_ref[ROWS : 2 * ROWS], 1.0)
-    y = butterfly([z[q * QUARTER : (q + 1) * QUARTER] for q in range(4)], 1.0)
-    y = quarter_dft(quarter_turns(y, turn_ref, 1.0), matrix_ref, 1.0)
+    pieces = split(x)
+    back, back_i = matrix_ref[BACK], matrix_ref[BACK_I]
+    pair = few_dft(pieces, [back, back]), few_dft(pieces, [back_i, back_i])
+    pair = turned_by(pair, turn_ref[:ROWS], turn_ref[ROWS : 2 * ROWS])
+    y = [tuple(one[q * QUARTER : (q + 1) * QUARTER] for one in pair) for q in range(4)]
+    y = quarter_turns(butterfly(y), turn_ref)
+    y = jnp.concatenate([jnp.concatenate(one, axis=0) for one in y], axis=1)
+    high, low = split(y)
+    last = matrix_ref[LAST]
+    wide = jnp.concatenate([last[:, :LANES], last[:, :LANES], last[:, LANES:]], axis=1)
+    found = dot(wide, jnp.concatenate([high, low, high], axis=0))
     for r in range(4):
-        out_ref[pl.ds(r, QUARTER, stride=4), :] = y[r] * scale
+        one = found[:, r * LANES : (r + 1) * LANES]
+        out_ref[pl.ds(r, QUARTER, stride=4), :] = one * scale
 
 
 def exchange(parts):
     group = lax.broadcasted_iota(jnp.int32, parts[0].shape, 1) // 8
     parts = list(parts)
-    for bit in range(4):
-        step = 1 << bit
-        keep = group // step % 2 == 0
+    for step in (1, 4):
+        digit = group // step % 4
+        masks = [digit == j for j in range(4)]
         for first in range(16):
-            if first & step:
+            if first // step % 4:
                 continue
-            a, b = parts[first], parts[first + step]
-            parts[first] = jnp.where(keep, a, pltpu.roll(b, 8 * step, 1))
-            parts[first + step] = jnp.where(keep, pltpu.roll(a, LANES - 8 * step, 1), b)
+            old = [parts[first + step * i] for i in range(4)]
+            for i in range(4):
+                one = old[i]
+                for j in range(4):
+                    if j != i:
+                        moved = pltpu.roll(old[j], (j - i) * 8 * step % LANES, 1)
+                        one = jnp.where(masks[j], moved, one)
+                parts[first + step * i] = one
     return parts
 
 
@@ -148,22 +167,31 @@
 def pack_kernel(count_ref, distance_ref, x_ref, first_ref, choice_ref, out_ref, held):
     for half in range(2):
         held[half] = x_ref[:, :, half * LANES : (half + 1) * LANES]
-        parts = [held[half, q // 8, pl.ds(q % 8, 8, stride=8), :] for q in range(16)]
-        for g, one in enumerate(exchange(parts)):
-            out_ref[half * 16 + g] = one
+    parts = []
+    for q in range(16):
+        some = [held[half, q // 8, pl.ds(q % 8, 8, stride=8), :] for half in range(2)]
+        parts.append(jnp.concatenate(some, axis=0))
+    for g, one in enumerate(exchange(parts)):
+        for half in range(2):
+            out_ref[half * 16 + g] = one[half * 8 : half * 8 + 8]
 
 
 def unpack_kernel(x_ref, out_ref, held, sems):
+    parts = [jnp.concatenate([x_ref[g], x_ref[16 + g]], axis=0) for g in range(16)]
     copies = []
-    for half in range(2):
-        for q, one in enumerate(exchange([x_ref[half * 16 + g] for g in range(16)])):
-            held[half, q // 8, pl.ds(q % 8, 8, stride=8), :] = one
-        copies.append(
-            pltpu.make_async_copy(
-                held.at[half], out_ref.at[:, :, pl.ds(half * LANES, LANES)], sems.at[half]
-            )
-        )
-        copies[half].start()
+    for q, one in enumerate(exchange(parts)):
+        for half in range(2):
+            held[half, q // 8, pl.ds(q % 8, 8, stride=8), :] = one[half * 8 : half * 8 + 8]
+        if q % 8 == 7:
+            for half in range(2):
+                copies.append(
+                    pltpu.make_async_copy(
+                        held.at[half, q // 8],
+                        out_ref.at[q // 8, :, pl.ds(half * LANES, LANES)],
+                        sems.at[q // 8 * 2 + half],
+                    )
+                )
+                copies[-1].start()
     for copy in copies:
         copy.wait()
 
@@ -193,8 +221,8 @@
     odd = halves_count - 2.0 * jnp.floor(0.5 * halves_count)
     sign = 1.0 - 2.0 * odd
     turn = 2.0 * math.pi
-    even_terms = [(-1) ** k * turn ** (2 * k) / math.factorial(2 * k) for k in range(8)]
-    odd_terms = [(-1) ** k * turn ** (2 * k + 1) / math.factorial(2 * k + 1) for k in range(7)]
+    even_terms = [(-1) ** k * turn ** (2 * k) / math.factorial(2 * k) for k in range(7)]
+    odd_terms = [(-1) ** k * turn ** (2 * k + 1) / math.factorial(2 * k + 1) for k in range(6)]
     square = rest * rest
     return sign * polynomial(square, even_terms), sign * rest * polynomial(square, odd_terms)
 
@@ -218,7 +246,7 @@
     fx = jnp.where(kx >= N // 2, kx - N, kx).astype(jnp.float32) * (1.0 / N)
     fr = jnp.where(kr >= N // 2, kr - N, kr).astype(jnp.float32) * (1.0 / N)
     cosine, sine = turn_tables(distance * jnp.sqrt((count + fr) ** 2 - 0.25 * fx**2))
-    return both_parts(cosine), both_parts(sine) * sign_row(1.0)
+    return both_parts(cosine), both_parts(sine)
 
 
 def lane_rows(rank, starts_ref, choice_ref):
@@ -244,6 +272,22 @@
     return starts, jnp.concatenate(chosen, axis=1)
 
 
+PER_LANE = lax.GatherDimensionNumbers(
+    offset_dims=(),
+    collapsed_slice_dims=(0,),
+    start_index_map=(0,),
+    operand_batching_dims=(1,),
+    start_indices_batching_dims=(1,),
+)
+PER_ROW = lax.GatherDimensionNumbers(
+    offset_dims=(),
+    collapsed_slice_dims=(1,),
+    start_index_map=(1,),
+    operand_batching_dims=(0,),
+    start_indices_batching_dims=(0,),
+)
+
+
 def write_bands(coef_ref, high_ref, low_ref):
     coef = coef_ref[...]
     columns = jnp.transpose(jnp.concatenate([coef, coef], axis=0))
@@ -251,10 +295,12 @@
     row = lax.broadcasted_iota(jnp.int32, (16, LANES), 0)
     for d in range(NW):
         slope = BLK + STRETCH * d
+        sloped = row * slope
         for g in range(BLK // 16):
             least = 16 * g * slope // BLK
             most = (16 * g + 15) * slope // BLK + TAPS - 1
-            start = (row + 16 * g) * slope // BLK
+            whole, rest = divmod(16 * g * slope, BLK)
+            start = (sloped + rest) >> 7
             rows = pl.ds(d * BLK + 16 * g, 16)
             for tile in range(2):
                 across = pl.ds(tile * LANES, LANES)
@@ -262,13 +308,16 @@
                     high_ref[rows, across] = jnp.zeros((16, LANES), jnp.bfloat16)
                     low_ref[rows, across] = jnp.zeros((16, LANES), jnp.bfloat16)
                     continue
-                ahead = lane + tile * LANES - start
-                inside = (ahead >= 0) & (ahead < TAPS)
-                at = jnp.where(inside, ahead, 0) + d * TAPS
-                taken = jnp.take_along_axis(
-                    columns[16 * g : 16 * g + 16], at, axis=1, mode="promise_in_bounds"
+                ahead = (lane + (tile * LANES - whole)) - start
+                tap = ahead & (TAPS - 1)
+                taken = lax.gather(
+                    columns[16 * g : 16 * g + 16],
+                    (tap | (d * TAPS))[:, :, None],
+                    PER_ROW,
+                    (1, 1),
+                    mode=lax.GatherScatterMode.PROMISE_IN_BOUNDS,
                 )
-                high, low = split(jnp.where(inside, taken, 0.0))
+                high, low = split(jnp.where(tap == ahead, taken, 0.0))
                 high_ref[rows, across] = high
                 low_ref[rows, across] = low
 
@@ -281,15 +330,26 @@
     for half in range(2):
         based = long[half * BLK : half * BLK + 3 * BLK]
         starts = all_starts[half]
-        for bit in reversed(range(8)):
+        for bit in reversed(range(3, 8)):
             step = 1 << bit
-            flagged = starts // step % 2 == 1
-            length = 2 * BLK + (step if step >= 8 else 8 if step > 1 else 0)
-            if step < 8:
-                moved = pltpu.roll(based, based.shape[0] - step, 0)
-            else:
-                moved = jnp.concatenate([based[step:], based[:step]], axis=0)
-            based = jnp.where(flagged, moved[:length], based[:length])
+            flagged = (starts >> bit) & 1 == 1
+            moved = jnp.concatenate([based[step:], based[:step]], axis=0)
+            based = jnp.where(flagged, moved, based)[: 2 * BLK + step]
+        fine = lax.broadcasted_iota(jnp.int32, (8, LANES), 0) + (starts & 7)
+        groups = [
+            lax.gather(
+                based[8 * g : 8 * g + 8],
+                (fine & 7)[:, :, None],
+                PER_LANE,
+                (1, 1),
+                mode=lax.GatherScatterMode.PROMISE_IN_BOUNDS,
+            )
+            for g in range(2 * BLK // 8 + 1)
+        ]
+        here = fine < 8
+        based = jnp.concatenate(
+            [jnp.where(here, groups[g], groups[g + 1]) for g in range(2 * BLK // 8)], axis=0
+        )
         high, low = split(based)
         highs.append(high)
         lows.append(low)
@@ -308,9 +368,9 @@
     out_ref, bh, bl,
 ):
     rank = own_rank()
-    lines = forward(x_ref, matrix_ref, turn_ref)
+    lines, side = forward(x_ref, matrix_ref, turn_ref, sides=True)
     cosine, sine = phase_tables(rank, count_ref[0], distance_ref[0])
-    turned = lines * cosine + swapped(lines) * sine
+    turned = lines * cosine + side * sine
     write_bands(coef_ref, bh, bl)
     starts, chosen = lane_rows(rank, starts_ref, choice_ref)
     focused = stolt(turned, bh, bl, starts, chosen)
@@ -366,7 +426,7 @@
     x = lax.all_to_all(x.reshape(32, 8, LANES), "pulse", 0, 0, tiled=True)
     return call(
         unpack_kernel, f32(2, 64, 256), x, outs=HBM,
-        scratch=[HELD, pltpu.SemaphoreType.DMA((2,))],
+        scratch=[HELD, pltpu.SemaphoreType.DMA((4,))],
     )
 
 

time: 80.1 us -> 78.7 us (0.983)
  Pallas kernels: 5.29 us -> 4.05 us
    pallas_call x6, Pallas kernels: 5.29 us -> 4.05 us  [call(): pl.pallas_call(kernel, out_shape=shapes, in_specs=[SMEM] * scalars + [VME...]
where the time goes in v2:
time: 78.7 us; the launch traced here: 78.5 us
  blocking collectives  72.9 us (93%)
  Pallas kernels  4.05 us (5%)
  between operations  1.44 us (2%)
    all_to_all x2, blocking collectives, local(): x = lax.all_to_all(x.reshape(ROWS, 1, LANES), whole, 0, 0, tiled=True)  38.9 us
    all_to_all x1, blocking collectives, local(): x = lax.all_to_all(x, 'pulse', 0, 0, tiled=True)  21.2 us
    all_to_all x1, blocking collectives, local(): x = lax.all_to_all(x.reshape(32, 8, LANES), 'pulse', 0, 0, tiled=True)  12.8 us
    pallas_call x6, Pallas kernels, call(): pl.pallas_call(kernel, out_shape=shapes, in_specs=[SMEM] * scalars + [VME...  4.05 us

profile of v2, /device:TPU:1, one launch (start us, length us, event | category | flops | bytes accessed | tf_op | source)
XLA Modules:
  0.0 78.5 jit_solution(15353307550724141701)
XLA Ops:
  0.0 0.0 copy-start
  0.7 0.0 copy-start.5
  1.4 0.0 copy-done.5
  1.4 0.0 copy-done
  1.4 0.0 copy-start.3
  1.4 0.0 copy-start.4
  1.4 0.3 shard_map.83
  1.7 21.2 %all_to_all.20 = f32[32,8,128]{2,1,0:T(8,128)S(1)} all-to-all(f32[32,8,128]{2,1,0:T(8,128)S(1)} %shard_map.83), channel_id=1, replica_groups=mesh['pulse'=32,'range'=8] {'pulse'}, dimensions={0} | all-to-all | bytes 262144 | tf_op jit(solution)/shard_map/all_to_all | solution.py:415
  22.9 0.0 copy-done.3
  22.9 0.0 copy-done.4
  22.9 0.4 shard_map.84
  23.4 0.0 copy-start.1
  23.4 0.0 copy-start.2
  23.4 20.7 %all_to_all.21 = f32[256,1,128]{2,1,0:T(1,128)S(1)} all-to-all(f32[256,1,128]{2,1,0:T(1,128)S(1)} %bitcast.19), channel_id=1, replica_groups=mesh['pulse'=32,'range'=8] {'range','pulse'}, dimensions={0} | all-to-all | bytes 262144 | tf_op jit(solution)/shard_map/all_to_all | solution.py:417
  44.1 0.0 copy-done.1
  44.1 0.0 copy-done.2
  44.1 1.9 %shard_map.85 = f32[256,128]{1,0:T(8,128)S(1)} custom-call(f32[1]{0:T(128)S(6)} %copy.11.count_ref, f32[1]{0:T(128)S(6)} %copy.12.distance_ref, f32[256,128]{1,0:T(8,128)S(1)} %bitcast.14, bf16[704,256]{1,0:T(8,128)(2,1)S(1)} %copy-done.4, f32[896,128]{1,0:T(8,128)S(1)} %copy-done.3, f32[1,16]{1,0:T(1,128)S(1)} %convert_bitcast_fusion.choice_ref, ...), custom_call_target="tpu_custom_call" | custom-call | flops 10000000000 | bytes 1048576 | tf_op jit(solution)/shard_map/pallas_call | solution.py:387
  45.9 18.3 %all_to_all.22 = f32[256,1,128]{2,1,0:T(1,128)S(1)} all-to-all(f32[256,1,128]{2,1,0:T(1,128)S(1)} %bitcast.15), channel_id=1, replica_groups=mesh['pulse'=32,'range'=8] {'range','pulse'}, dimensions={0} | all-to-all | bytes 262144 | tf_op jit(solution)/shard_map/all_to_all | solution.py:424
  64.2 0.5 shard_map.86
  64.7 12.8 %all_to_all.23.x_ref = f32[32,8,128]{2,1,0:T(8,128)S(1)} all-to-all(f32[32,8,128]{2,1,0:T(8,128)S(1)} %bitcast.17), channel_id=1, replica_groups=mesh['pulse'=32,'range'=8] {'pulse'}, dimensions={0} | all-to-all | bytes 262144 | tf_op jit(solution)/shard_map/all_to_all | solution.py:426
  77.5 1.0 %shard_map.87 = f32[2,64,256]{2,1,0:T(8,128)} custom-call(f32[32,8,128]{2,1,0:T(8,128)S(1)} %all_to_all.23.x_ref), custom_call_target="tpu_custom_call" | custom-call | flops 10000000000 | bytes 1048576 | tf_op jit(solution)/shard_map/pallas_call | solution.py:387
  (2 shorter events, 0.0 us)
Async XLA Ops:
  0.0 1.4 %copy-start = (f32[2,64,256]{2,1,0:T(8,128)S(1)}, f32[2,64,256]{2,1,0:T(8,128)}, u32[]{:S(2)}) copy-start(f32[2,64,256]{2,1,0:T(8,128)} %x_ref.1) | copy-start | bytes 393220
  0.7 0.7 copy-start.5
  1.4 21.5 %copy-start.3 = (f32[896,128]{1,0:T(8,128)S(1)}, f32[896,128]{1,0:T(8,128)}, u32[]{:S(2)}) copy-start(f32[896,128]{1,0:T(8,128)} %constant.5.clone.turn_ref) | copy-start | bytes 1376260
  1.4 21.5 %copy-start.4 = (bf16[704,256]{1,0:T(8,128)(2,1)S(1)}, bf16[704,256]{1,0:T(8,128)(2,1)}, u32[]{:S(2)}) copy-start(bf16[704,256]{1,0:T(8,128)(2,1)} %constant.4.clone.matrix_ref) | copy-start | bytes 1081348
  23.4 20.7 %copy-start.1 = (s32[2048,16]{0,1:T(8,128)S(1)}, s32[2048,16]{0,1:T(8,128)}, u32[]{:S(2)}) copy-start(s32[2048,16]{0,1:T(8,128)} %param.11) | copy-start | bytes 393220
  23.4 20.7 %copy-start.2 = (f32[8,8,128]{2,1,0:T(8,128)S(1)}, f32[8,8,128]{2,1,0:T(8,128)}, u32[]{:S(2)}) copy-start(f32[8,8,128]{2,1,0:T(8,128)} %param.13) | copy-start | bytes 98308

commit v3 on v2

--- a/solution.py
+++ b/solution.py
@@ -160,11 +160,7 @@
     return parts
 
 
-def first_kernel(out_ref):
-    out_ref[...] = jnp.zeros_like(out_ref)
-
-
-def pack_kernel(count_ref, distance_ref, x_ref, first_ref, choice_ref, out_ref, held):
+def pack_kernel(x_ref, out_ref, held):
     for half in range(2):
         held[half] = x_ref[:, :, half * LANES : (half + 1) * LANES]
     parts = []
@@ -196,7 +192,7 @@
         copy.wait()
 
 
-def azimuth_kernel(x_ref, matrix_ref, turn_ref, out_ref):
+def azimuth_kernel(x_ref, matrix_ref, turn_ref, lane_ref, out_ref):
     out_ref[...] = forward(x_ref, matrix_ref, turn_ref)
 
 
@@ -363,16 +359,24 @@
     return jnp.concatenate([result[:, :LANES], result[:, LANES:]], axis=0)
 
 
-def range_kernel(
-    count_ref, distance_ref, x_ref, matrix_ref, turn_ref, choice_ref, starts_ref, coef_ref,
-    out_ref, bh, bl,
+def prepare_kernel(
+    count_ref, distance_ref, choice_ref, starts_ref, coef_ref, phase_ref, bh, bl, lane_ref
 ):
     rank = own_rank()
-    lines, side = forward(x_ref, matrix_ref, turn_ref, sides=True)
-    cosine, sine = phase_tables(rank, count_ref[0], distance_ref[0])
-    turned = lines * cosine + side * sine
+    phase_ref[:ROWS], phase_ref[ROWS:] = phase_tables(rank, count_ref[0], distance_ref[0])
     write_bands(coef_ref, bh, bl)
     starts, chosen = lane_rows(rank, starts_ref, choice_ref)
+    for half in range(2):
+        lane_ref[half : half + 1, :] = starts[half]
+        lane_ref[2 + half : 3 + half, :] = chosen[:, half * LANES : (half + 1) * LANES]
+    lane_ref[4:8, :] = jnp.zeros((4, LANES), jnp.int32)
+
+
+def range_kernel(x_ref, matrix_ref, turn_ref, phase_ref, bh, bl, lane_ref, out_ref):
+    lines, side = forward(x_ref, matrix_ref, turn_ref, sides=True)
+    turned = lines * phase_ref[:ROWS] + side * phase_ref[ROWS:]
+    starts = [lane_ref[0:1, :], lane_ref[1:2, :]]
+    chosen = jnp.concatenate([lane_ref[2:3, :], lane_ref[3:4, :]], axis=1)
     focused = stolt(turned, bh, bl, starts, chosen)
     inverse(focused, matrix_ref, turn_ref, out_ref)
 
@@ -388,7 +392,7 @@
         kernel,
         out_shape=shapes,
         in_specs=[SMEM] * scalars + [VMEM] * (len(args) - scalars),
-        out_specs=jax.tree.map(lambda _: outs, shapes),
+        out_specs=[outs] * len(shapes) if isinstance(shapes, tuple) else outs,
         scratch_shapes=scratch,
         compiler_params=pltpu.CompilerParams(vmem_limit_bytes=32 * 2**20),
         cost_estimate=pl.CostEstimate(flops=10**10, bytes_accessed=2**20, transcendentals=0),
@@ -406,21 +410,19 @@
 def local(returns, center, distance, starts, choices, coefficients):
     whole = ("range", "pulse")
     known = tables()
-    choices = choices.astype(jnp.float32).reshape(1, 16)
-    first = call(first_kernel, f32(8, LANES))
-    x = call(
-        pack_kernel, f32(32, 8, LANES), center, distance, returns, first, choices,
-        scalars=2, scratch=[HELD],
+    bands = bf16(NW * BLK, 2 * BLK)
+    prepared = call(
+        prepare_kernel,
+        (f32(2 * ROWS, LANES), bands, bands, jax.ShapeDtypeStruct((8, LANES), jnp.int32)),
+        center, distance, choices.astype(jnp.float32).reshape(1, 16), starts.T,
+        coefficients.reshape(NW * TAPS, BLK),
+        scalars=2,
     )
+    x = call(pack_kernel, f32(32, 8, LANES), returns, scratch=[HELD])
     x = lax.all_to_all(x, "pulse", 0, 0, tiled=True)
-    x = call(azimuth_kernel, f32(ROWS, LANES), x.reshape(ROWS, LANES), *known)
+    x = call(azimuth_kernel, f32(ROWS, LANES), x.reshape(ROWS, LANES), *known, prepared[-1])
     x = lax.all_to_all(x.reshape(ROWS, 1, LANES), whole, 0, 0, tiled=True)
-    x = call(
-        range_kernel, f32(ROWS, LANES), center, distance, x.reshape(ROWS, LANES), *known,
-        choices, starts.T, coefficients.reshape(NW * TAPS, BLK),
-        scalars=2,
-        scratch=[pltpu.VMEM((NW * BLK, 2 * BLK), jnp.bfloat16)] * 2,
-    )
+    x = call(range_kernel, f32(ROWS, LANES), x.reshape(ROWS, LANES), *known, *prepared)
     x = lax.all_to_all(x.reshape(ROWS, 1, LANES), whole, 0, 0, tiled=True)
     x = call(azimuth_back_kernel, f32(ROWS, LANES), x.reshape(ROWS, LANES), *known)
     x = lax.all_to_all(x.reshape(32, 8, LANES), "pulse", 0, 0, tiled=True)

time: 78.7 us -> 78.8 us (level)
  blocking collectives: 72.9 us -> 51.7 us
  starting transfers between devices: 0 us -> 12.2 us
  waiting for transfers between devices: 0 us -> 7.23 us
  Pallas kernels: 4.05 us -> 5.06 us
  local copies, waits for them, and re-layouts: 0.04 us -> 0.93 us
    all_to_all x1 -> x0, blocking collectives: 21.2 us -> none  [local(): x = lax.all_to_all(x, 'pulse', 0, 0, tiled=True)]
    all_to_all x0 -> x1, starting transfers between devices: none -> 12.2 us  [local(): x = lax.all_to_all(x, 'pulse', 0, 0, tiled=True)]
    all_to_all x0 -> x1, waiting for transfers between devices: none -> 7.23 us  [local(): x = lax.all_to_all(x, 'pulse', 0, 0, tiled=True)]
    pallas_call x6, Pallas kernels: 4.05 us -> 5.06 us  [call(): pl.pallas_call(kernel, out_shape=shapes, in_specs=[SMEM] * scalars + [VME...]
    unnamed x12, local copies, waits for them, and re-layouts: 0.04 us -> 0.93 us
  transfers between devices with their start and end apart: 0 -> 1, of which waited for: 0 -> 1; matrix products, arithmetic and copies ran while one was open for 0% -> 0% of each run, Pallas kernels for 0% -> 1%
where the time goes in v3:
time: 78.8 us; the launch traced here: 78.5 us
  blocking collectives  51.7 us (66%)
  starting transfers between devices  12.2 us (15%)
  waiting for transfers between devices  7.23 us (9%)
  Pallas kernels  5.06 us (6%)
  between operations  1.4 us (2%)
  local copies, waits for them, and re-layouts  0.93 us (1%)
    all_to_all x2, blocking collectives, local(): x = lax.all_to_all(x.reshape(ROWS, 1, LANES), whole, 0, 0, tiled=True)  39 us
    all_to_all x1, blocking collectives, local(): x = lax.all_to_all(x.reshape(32, 8, LANES), 'pulse', 0, 0, tiled=True)  12.8 us
    all_to_all x1, starting transfers between devices, local(): x = lax.all_to_all(x, 'pulse', 0, 0, tiled=True)  12.2 us
    all_to_all x1, waiting for transfers between devices, local(): x = lax.all_to_all(x, 'pulse', 0, 0, tiled=True)  7.23 us
    pallas_call x6, Pallas kernels, call(): pl.pallas_call(kernel, out_shape=shapes, in_specs=[SMEM] * scalars + [VME...  5.06 us
  transfers between devices with their start and end apart: 1, of which 1 were waited for; matrix products, arithmetic and copies ran while one was open for 0% of the time, Pallas kernels for 1%

profile of v3, /device:TPU:1, one launch (start us, length us, event | category | flops | bytes accessed | tf_op | source)
XLA Modules:
  0.0 78.5 jit_solution(17124182940173818818)
XLA Ops:
  0.0 0.0 copy-start
  0.0 0.9 %copy-done = f32[2,64,256]{2,1,0:T(8,128)S(1)} copy-done((f32[2,64,256]{2,1,0:T(8,128)S(1)}, f32[2,64,256]{2,1,0:T(8,128)}, u32[]{:S(2)}) %copy-start) | copy-done | bytes 131096
  0.9 1.0 %shard_map.82 = f32[32,8,128]{2,1,0:T(8,128)} custom-call(f32[2,64,256]{2,1,0:T(8,128)S(1)} %copy-done), custom_call_target="tpu_custom_call" | custom-call | flops 10000000000 | bytes 1048576 | tf_op jit(solution)/shard_map/pallas_call | solution.py:391
  1.9 0.0 copy-start.1
  1.9 0.0 copy-start.2
  1.9 12.2 %all-to-all-start = ((f32[32,8,128]{2,1,0:T(8,128)}), f32[32,8,128]{2,1,0:T(8,128)S(1)}, u32[]{:S(2)}, u32[]{:S(2)}) async-start(f32[32,8,128]{2,1,0:T(8,128)} %shard_map.82), calls=%async_computation | async-start | bytes 262144 | tf_op jit(solution)/shard_map/all_to_all | solution.py:422
  14.7 0.0 copy-start.5
  15.4 0.0 copy-done.5
  15.4 0.0 copy-done.1
  15.4 0.0 copy-done.2
  15.4 0.0 copy-start.3
  15.4 0.0 copy-start.4
  15.4 0.7 shard_map.83
  16.2 7.2 %all-to-all-done = f32[32,8,128]{2,1,0:T(8,128)S(1)} async-done(((f32[32,8,128]{2,1,0:T(8,128)}), f32[32,8,128]{2,1,0:T(8,128)S(1)}, u32[]{:S(2)}, u32[]{:S(2)}) %all-to-all-start) | async-done | bytes 131104 | tf_op jit(solution)/shard_map/all_to_all | solution.py:422
  23.4 0.0 copy-done.3
  23.4 0.0 copy-done.4
  23.4 0.4 shard_map.84
  23.8 20.7 %all_to_all.20 = f32[256,1,128]{2,1,0:T(1,128)S(1)} all-to-all(f32[256,1,128]{2,1,0:T(1,128)S(1)} %bitcast.19), channel_id=1, replica_groups=mesh['pulse'=32,'range'=8] {'range','pulse'}, dimensions={0} | all-to-all | bytes 262144 | tf_op jit(solution)/shard_map/all_to_all | solution.py:424
  44.5 1.5 %shard_map.85 = f32[256,128]{1,0:T(8,128)S(1)} custom-call(f32[256,128]{1,0:T(8,128)S(1)} %bitcast.15, bf16[704,256]{1,0:T(8,128)(2,1)S(1)} %copy-done.4, f32[896,128]{1,0:T(8,128)S(1)} %copy-done.3, f32[512,128]{1,0:T(8,128)S(1)} %get-tuple-element.10.phase_ref, bf16[1024,256]{1,0:T(8,128)(2,1)S(1)} %get-tuple-element.11.bh, ...), custom_call_target="tpu_custom_call" | custom-call | flops 10000000000 | bytes 1048576 | tf_op jit(solution)/shard_map/pallas_call | solution.py:391
  46.0 18.3 %all_to_all.21 = f32[256,1,128]{2,1,0:T(1,128)S(1)} all-to-all(f32[256,1,128]{2,1,0:T(1,128)S(1)} %bitcast.16), channel_id=1, replica_groups=mesh['pulse'=32,'range'=8] {'range','pulse'}, dimensions={0} | all-to-all | bytes 262144 | tf_op jit(solution)/shard_map/all_to_all | solution.py:426
  64.3 0.5 shard_map.86
  64.8 12.8 %all_to_all.22.x_ref = f32[32,8,128]{2,1,0:T(8,128)S(1)} all-to-all(f32[32,8,128]{2,1,0:T(8,128)S(1)} %bitcast.18), channel_id=1, replica_groups=mesh['pulse'=32,'range'=8] {'pulse'}, dimensions={0} | all-to-all | bytes 262144 | tf_op jit(solution)/shard_map/all_to_all | solution.py:428
  77.6 1.0 %shard_map.87 = f32[2,64,256]{2,1,0:T(8,128)} custom-call(f32[32,8,128]{2,1,0:T(8,128)S(1)} %all_to_all.22.x_ref), custom_call_target="tpu_custom_call" | custom-call | flops 10000000000 | bytes 1048576 | tf_op jit(solution)/shard_map/pallas_call | solution.py:391
  (1 shorter events, 0.0 us)
Async XLA Ops:
  0.0 0.9 %copy-start = (f32[2,64,256]{2,1,0:T(8,128)S(1)}, f32[2,64,256]{2,1,0:T(8,128)}, u32[]{:S(2)}) copy-start(f32[2,64,256]{2,1,0:T(8,128)} %x_ref.1) | copy-start | bytes 393220
  1.9 13.5 %copy-start.1 = (s32[2048,16]{0,1:T(8,128)S(1)}, s32[2048,16]{0,1:T(8,128)}, u32[]{:S(2)}) copy-start(s32[2048,16]{0,1:T(8,128)} %param.11) | copy-start | bytes 393220
  1.9 13.5 %copy-start.2 = (f32[8,8,128]{2,1,0:T(8,128)S(1)}, f32[8,8,128]{2,1,0:T(8,128)}, u32[]{:S(2)}) copy-start(f32[8,8,128]{2,1,0:T(8,128)} %param.13) | copy-start | bytes 98308
  1.9 21.5 %all-to-all-start = ((f32[32,8,128]{2,1,0:T(8,128)}), f32[32,8,128]{2,1,0:T(8,128)S(1)}, u32[]{:S(2)}, u32[]{:S(2)}) async-start(f32[32,8,128]{2,1,0:T(8,128)} %shard_map.82), calls=%async_computation | async-start | bytes 262144 | tf_op jit(solution)/shard_map/all_to_all | solution.py:422
  14.7 0.7 copy-start.5
  15.4 8.0 %copy-start.3 = (f32[896,128]{1,0:T(8,128)S(1)}, f32[896,128]{1,0:T(8,128)}, u32[]{:S(2)}) copy-start(f32[896,128]{1,0:T(8,128)} %constant.5.clone.turn_ref) | copy-start | bytes 1376260
  15.4 8.0 %copy-start.4 = (bf16[704,256]{1,0:T(8,128)(2,1)S(1)}, bf16[704,256]{1,0:T(8,128)(2,1)}, u32[]{:S(2)}) copy-start(bf16[704,256]{1,0:T(8,128)(2,1)} %constant.4.clone.matrix_ref) | copy-start | bytes 1081348

commit v4 on v2

--- a/solution.py
+++ b/solution.py
@@ -104,6 +104,13 @@
     return both[:, :LANES] + both[:, LANES:] * math.sqrt(0.5)
 
 
+def few_dft_both(x, table, table_i):
+    table = jnp.concatenate([table, table_i], axis=1)
+    both = dot(jnp.concatenate(x, axis=1), jnp.concatenate([table, table], axis=0))
+    parts = [both[:, at * LANES : (at + 1) * LANES] for at in range(4)]
+    return [parts[at] + parts[at + 1] * math.sqrt(0.5) for at in (0, 2)]
+
+
 def forward(x_ref, matrix_ref, turn_ref, sides=False):
     x = jnp.concatenate([x_ref[pl.ds(r, QUARTER, stride=4), :] for r in range(4)], axis=1)
     high, low = split(x)
@@ -120,13 +127,13 @@
         return few_dft([*split(a), *split(b)], [into, into, into_i, into_i])
     lane = lax.broadcasted_iota(jnp.int32, (1, LANES), 1)
     pieces = split(a + swapped(b * jnp.where(lane < LANES // 2, 1.0, -1.0)))
-    return few_dft(pieces, [into, into]), few_dft(pieces, [into_i, into_i])
+    return few_dft_both(pieces, into, into_i)
 
 
 def inverse(x, matrix_ref, turn_ref, out_ref, scale=1.0):
     pieces = split(x)
     back, back_i = matrix_ref[BACK], matrix_ref[BACK_I]
-    pair = few_dft(pieces, [back, back]), few_dft(pieces, [back_i, back_i])
+    pair = few_dft_both(pieces, back, back_i)
     pair = turned_by(pair, turn_ref[:ROWS], turn_ref[ROWS : 2 * ROWS])
     y = [tuple(one[q * QUARTER : (q + 1) * QUARTER] for one in pair) for q in range(4)]
     y = quarter_turns(butterfly(y), turn_ref)
@@ -288,36 +295,44 @@
 )
 
 
+def per_row(rows, at):
+    return lax.gather(
+        rows, at[:, :, None], PER_ROW, (1, 1), mode=lax.GatherScatterMode.PROMISE_IN_BOUNDS
+    )
+
+
 def write_bands(coef_ref, high_ref, low_ref):
     coef = coef_ref[...]
     columns = jnp.transpose(jnp.concatenate([coef, coef], axis=0))
-    lane = lax.broadcasted_iota(jnp.int32, (16, LANES), 1)
-    row = lax.broadcasted_iota(jnp.int32, (16, LANES), 0)
+    lane = lax.broadcasted_iota(jnp.int32, (8, LANES), 1)
+    row = lax.broadcasted_iota(jnp.int32, (8, LANES), 0)
+    slopes = BLK + STRETCH * ((lane >> 3) & (NW - 1))
+    turned = []
+    for first in range(0, BLK, 8):
+        start = ((row + first) * slopes) >> 7
+        at = (lane & -TAPS) | ((lane - start) & (TAPS - 1))
+        turned.append(per_row(columns[first : first + 8], at))
     for d in range(NW):
         slope = BLK + STRETCH * d
         sloped = row * slope
+        repeat = (lane & (TAPS - 1)) | (d * TAPS)
         for g in range(BLK // 16):
-            least = 16 * g * slope // BLK
-            most = (16 * g + 15) * slope // BLK + TAPS - 1
-            whole, rest = divmod(16 * g * slope, BLK)
-            start = (sloped + rest) >> 7
+            pieces = [[], []]
+            for first in (16 * g, 16 * g + 8):
+                whole, rest = divmod(first * slope, BLK)
+                most = (first + 7) * slope // BLK + TAPS - 1
+                start = (sloped + rest) >> 7
+                taken = per_row(turned[first // 8], repeat)
+                for tile in range(2):
+                    if whole >= (tile + 1) * LANES or most < tile * LANES:
+                        pieces[tile].append(jnp.zeros((8, LANES), jnp.float32))
+                        continue
+                    ahead = (lane + (tile * LANES - whole)) - start
+                    pieces[tile].append(jnp.where((ahead & -TAPS) == 0, taken, 0.0))
             rows = pl.ds(d * BLK + 16 * g, 16)
             for tile in range(2):
                 across = pl.ds(tile * LANES, LANES)
-                if least >= (tile + 1) * LANES or most < tile * LANES:
-                    high_ref[rows, across] = jnp.zeros((16, LANES), jnp.bfloat16)
-                    low_ref[rows, across] = jnp.zeros((16, LANES), jnp.bfloat16)
-                    continue
-                ahead = (lane + (tile * LANES - whole)) - start
-                tap = ahead & (TAPS - 1)
-                taken = lax.gather(
-                    columns[16 * g : 16 * g + 16],
-                    (tap | (d * TAPS))[:, :, None],
-                    PER_ROW,
-                    (1, 1),
-                    mode=lax.GatherScatterMode.PROMISE_IN_BOUNDS,
-                )
-                high, low = split(jnp.where(tap == ahead, taken, 0.0))
+                high, low = split(jnp.concatenate(pieces[tile], axis=0))
                 high_ref[rows, across] = high
                 low_ref[rows, across] = low
 

time: 78.7 us -> 78.5 us (level)
  no operation moved by 1% of the time
where the time goes in v4:
time: 78.5 us; the launch traced here: 78.3 us
  blocking collectives  72.9 us (93%)
  Pallas kernels  3.89 us (5%)
  between operations  1.44 us (2%)
    all_to_all x2, blocking collectives, local(): x = lax.all_to_all(x.reshape(ROWS, 1, LANES), whole, 0, 0, tiled=True)  38.9 us
    all_to_all x1, blocking collectives, local(): x = lax.all_to_all(x, 'pulse', 0, 0, tiled=True)  21.2 us
    all_to_all x1, blocking collectives, local(): x = lax.all_to_all(x.reshape(32, 8, LANES), 'pulse', 0, 0, tiled=True)  12.8 us
    pallas_call x6, Pallas kernels, call(): pl.pallas_call(kernel, out_shape=shapes, in_specs=[SMEM] * scalars + [VME...  3.89 us

profile of v4, /device:TPU:1, one launch (start us, length us, event | category | flops | bytes accessed | tf_op | source)
XLA Modules:
  0.0 78.3 jit_solution(12904325214483281181)
XLA Ops:
  0.0 0.0 copy-start
  0.7 0.0 copy-start.5
  1.4 0.0 copy-done.5
  1.4 0.0 copy-done
  1.4 0.0 copy-start.3
  1.4 0.0 copy-start.4
  1.4 0.3 shard_map.83
  1.7 21.2 %all_to_all.20 = f32[32,8,128]{2,1,0:T(8,128)S(1)} all-to-all(f32[32,8,128]{2,1,0:T(8,128)S(1)} %shard_map.83), channel_id=1, replica_groups=mesh['pulse'=32,'range'=8] {'pulse'}, dimensions={0} | all-to-all | bytes 262144 | tf_op jit(solution)/shard_map/all_to_all | solution.py:430
  22.9 0.0 copy-done.3
  22.9 0.0 copy-done.4
  22.9 0.4 shard_map.84
  23.4 0.0 copy-start.1
  23.4 0.0 copy-start.2
  23.4 20.7 %all_to_all.21 = f32[256,1,128]{2,1,0:T(1,128)S(1)} all-to-all(f32[256,1,128]{2,1,0:T(1,128)S(1)} %bitcast.19), channel_id=1, replica_groups=mesh['pulse'=32,'range'=8] {'range','pulse'}, dimensions={0} | all-to-all | bytes 262144 | tf_op jit(solution)/shard_map/all_to_all | solution.py:432
  44.1 0.0 copy-done.1
  44.1 0.0 copy-done.2
  44.1 1.7 %shard_map.85 = f32[256,128]{1,0:T(8,128)S(1)} custom-call(f32[1]{0:T(128)S(6)} %copy.11.count_ref, f32[1]{0:T(128)S(6)} %copy.12.distance_ref, f32[256,128]{1,0:T(8,128)S(1)} %bitcast.14, bf16[704,256]{1,0:T(8,128)(2,1)S(1)} %copy-done.4, f32[896,128]{1,0:T(8,128)S(1)} %copy-done.3, f32[1,16]{1,0:T(1,128)S(1)} %convert_bitcast_fusion.choice_ref, ...), custom_call_target="tpu_custom_call" | custom-call | flops 10000000000 | bytes 1048576 | tf_op jit(solution)/shard_map/pallas_call | solution.py:402
  45.8 18.3 %all_to_all.22 = f32[256,1,128]{2,1,0:T(1,128)S(1)} all-to-all(f32[256,1,128]{2,1,0:T(1,128)S(1)} %bitcast.15), channel_id=1, replica_groups=mesh['pulse'=32,'range'=8] {'range','pulse'}, dimensions={0} | all-to-all | bytes 262144 | tf_op jit(solution)/shard_map/all_to_all | solution.py:439
  64.1 0.5 shard_map.86
  64.5 12.8 %all_to_all.23.x_ref = f32[32,8,128]{2,1,0:T(8,128)S(1)} all-to-all(f32[32,8,128]{2,1,0:T(8,128)S(1)} %bitcast.17), channel_id=1, replica_groups=mesh['pulse'=32,'range'=8] {'pulse'}, dimensions={0} | all-to-all | bytes 262144 | tf_op jit(solution)/shard_map/all_to_all | solution.py:441
  77.3 1.0 %shard_map.87 = f32[2,64,256]{2,1,0:T(8,128)} custom-call(f32[32,8,128]{2,1,0:T(8,128)S(1)} %all_to_all.23.x_ref), custom_call_target="tpu_custom_call" | custom-call | flops 10000000000 | bytes 1048576 | tf_op jit(solution)/shard_map/pallas_call | solution.py:402
  (2 shorter events, 0.0 us)
Async XLA Ops:
  0.0 1.4 %copy-start = (f32[2,64,256]{2,1,0:T(8,128)S(1)}, f32[2,64,256]{2,1,0:T(8,128)}, u32[]{:S(2)}) copy-start(f32[2,64,256]{2,1,0:T(8,128)} %x_ref.1) | copy-start | bytes 393220
  0.7 0.7 copy-start.5
  1.4 21.5 %copy-start.3 = (f32[896,128]{1,0:T(8,128)S(1)}, f32[896,128]{1,0:T(8,128)}, u32[]{:S(2)}) copy-start(f32[896,128]{1,0:T(8,128)} %constant.5.clone.turn_ref) | copy-start | bytes 1376260
  1.4 21.5 %copy-start.4 = (bf16[704,256]{1,0:T(8,128)(2,1)S(1)}, bf16[704,256]{1,0:T(8,128)(2,1)}, u32[]{:S(2)}) copy-start(bf16[704,256]{1,0:T(8,128)(2,1)} %constant.4.clone.matrix_ref) | copy-start | bytes 1081348
  23.4 20.7 %copy-start.1 = (s32[2048,16]{0,1:T(8,128)S(1)}, s32[2048,16]{0,1:T(8,128)}, u32[]{:S(2)}) copy-start(s32[2048,16]{0,1:T(8,128)} %param.11) | copy-start | bytes 393220
  23.4 20.7 %copy-start.2 = (f32[8,8,128]{2,1,0:T(8,128)S(1)}, f32[8,8,128]{2,1,0:T(8,128)}, u32[]{:S(2)}) copy-start(f32[8,8,128]{2,1,0:T(8,128)} %param.13) | copy-start | bytes 98308

commit v5 on v4

--- a/solution.py
+++ b/solution.py
@@ -125,9 +125,12 @@
     into, into_i = matrix_ref[INTO], matrix_ref[INTO_I]
     if not sides:
         return few_dft([*split(a), *split(b)], [into, into, into_i, into_i])
-    lane = lax.broadcasted_iota(jnp.int32, (1, LANES), 1)
-    pieces = split(a + swapped(b * jnp.where(lane < LANES // 2, 1.0, -1.0)))
-    return few_dft_both(pieces, into, into_i)
+    pieces = [*split(a), *split(b)]
+    table = jnp.concatenate([into, into, into_i, into_i], axis=0)
+    table_i = jnp.concatenate([into_i, into_i, -into, -into], axis=0)
+    both = dot(jnp.concatenate(pieces, axis=1), jnp.concatenate([table, table_i], axis=1))
+    parts = [both[:, at * LANES : (at + 1) * LANES] for at in range(4)]
+    return [parts[at] + parts[at + 1] * math.sqrt(0.5) for at in (0, 2)]
 
 
 def inverse(x, matrix_ref, turn_ref, out_ref, scale=1.0):

time: 78.5 us -> 78.5 us (level)
  no operation moved by 1% of the time
where the time goes in v5:
time: 78.5 us; the launch traced here: 78.3 us
  blocking collectives  72.9 us (93%)
  Pallas kernels  3.87 us (5%)
  between operations  1.44 us (2%)
    all_to_all x2, blocking collectives, local(): x = lax.all_to_all(x.reshape(ROWS, 1, LANES), whole, 0, 0, tiled=True)  39 us
    all_to_all x1, blocking collectives, local(): x = lax.all_to_all(x, 'pulse', 0, 0, tiled=True)  21.2 us
    all_to_all x1, blocking collectives, local(): x = lax.all_to_all(x.reshape(32, 8, LANES), 'pulse', 0, 0, tiled=True)  12.8 us
    pallas_call x6, Pallas kernels, call(): pl.pallas_call(kernel, out_shape=shapes, in_specs=[SMEM] * scalars + [VME...  3.87 us

profile of v5, /device:TPU:1, one launch (start us, length us, event | category | flops | bytes accessed | tf_op | source)
XLA Modules:
  0.0 78.3 jit_solution(14287996681910622328)
XLA Ops:
  0.0 0.0 copy-start
  0.7 0.0 copy-start.5
  1.4 0.0 copy-done.5
  1.4 0.0 copy-done
  1.4 0.0 copy-start.3
  1.4 0.0 copy-start.4
  1.4 0.3 shard_map.83
  1.7 21.2 %all_to_all.20 = f32[32,8,128]{2,1,0:T(8,128)S(1)} all-to-all(f32[32,8,128]{2,1,0:T(8,128)S(1)} %shard_map.83), channel_id=1, replica_groups=mesh['pulse'=32,'range'=8] {'pulse'}, dimensions={0} | all-to-all | bytes 262144 | tf_op jit(solution)/shard_map/all_to_all | solution.py:433
  22.9 0.0 copy-done.3
  22.9 0.0 copy-done.4
  22.9 0.4 shard_map.84
  23.4 0.0 copy-start.1
  23.4 0.0 copy-start.2
  23.4 20.7 %all_to_all.21 = f32[256,1,128]{2,1,0:T(1,128)S(1)} all-to-all(f32[256,1,128]{2,1,0:T(1,128)S(1)} %bitcast.19), channel_id=1, replica_groups=mesh['pulse'=32,'range'=8] {'range','pulse'}, dimensions={0} | all-to-all | bytes 262144 | tf_op jit(solution)/shard_map/all_to_all | solution.py:435
  44.1 0.0 copy-done.1
  44.1 0.0 copy-done.2
  44.1 1.7 %shard_map.85 = f32[256,128]{1,0:T(8,128)S(1)} custom-call(f32[1]{0:T(128)S(6)} %copy.11.count_ref, f32[1]{0:T(128)S(6)} %copy.12.distance_ref, f32[256,128]{1,0:T(8,128)S(1)} %bitcast.14, bf16[704,256]{1,0:T(8,128)(2,1)S(1)} %copy-done.4, f32[896,128]{1,0:T(8,128)S(1)} %copy-done.3, f32[1,16]{1,0:T(1,128)S(1)} %convert_bitcast_fusion.choice_ref, ...), custom_call_target="tpu_custom_call" | custom-call | flops 10000000000 | bytes 1048576 | tf_op jit(solution)/shard_map/pallas_call | solution.py:405
  45.8 18.3 %all_to_all.22 = f32[256,1,128]{2,1,0:T(1,128)S(1)} all-to-all(f32[256,1,128]{2,1,0:T(1,128)S(1)} %bitcast.15), channel_id=1, replica_groups=mesh['pulse'=32,'range'=8] {'range','pulse'}, dimensions={0} | all-to-all | bytes 262144 | tf_op jit(solution)/shard_map/all_to_all | solution.py:442
  64.1 0.5 shard_map.86
  64.5 12.8 %all_to_all.23.x_ref = f32[32,8,128]{2,1,0:T(8,128)S(1)} all-to-all(f32[32,8,128]{2,1,0:T(8,128)S(1)} %bitcast.17), channel_id=1, replica_groups=mesh['pulse'=32,'range'=8] {'pulse'}, dimensions={0} | all-to-all | bytes 262144 | tf_op jit(solution)/shard_map/all_to_all | solution.py:444
  77.3 1.0 %shard_map.87 = f32[2,64,256]{2,1,0:T(8,128)} custom-call(f32[32,8,128]{2,1,0:T(8,128)S(1)} %all_to_all.23.x_ref), custom_call_target="tpu_custom_call" | custom-call | flops 10000000000 | bytes 1048576 | tf_op jit(solution)/shard_map/pallas_call | solution.py:405
  (2 shorter events, 0.0 us)
Async XLA Ops:
  0.0 1.4 %copy-start = (f32[2,64,256]{2,1,0:T(8,128)S(1)}, f32[2,64,256]{2,1,0:T(8,128)}, u32[]{:S(2)}) copy-start(f32[2,64,256]{2,1,0:T(8,128)} %x_ref.1) | copy-start | bytes 393220
  0.7 0.7 copy-start.5
  1.4 21.5 %copy-start.3 = (f32[896,128]{1,0:T(8,128)S(1)}, f32[896,128]{1,0:T(8,128)}, u32[]{:S(2)}) copy-start(f32[896,128]{1,0:T(8,128)} %constant.5.clone.turn_ref) | copy-start | bytes 1376260
  1.4 21.5 %copy-start.4 = (bf16[704,256]{1,0:T(8,128)(2,1)S(1)}, bf16[704,256]{1,0:T(8,128)(2,1)}, u32[]{:S(2)}) copy-start(bf16[704,256]{1,0:T(8,128)(2,1)} %constant.4.clone.matrix_ref) | copy-start | bytes 1081348
  23.4 20.7 %copy-start.1 = (s32[2048,16]{0,1:T(8,128)S(1)}, s32[2048,16]{0,1:T(8,128)}, u32[]{:S(2)}) copy-start(s32[2048,16]{0,1:T(8,128)} %param.11) | copy-start | bytes 393220
  23.4 20.7 %copy-start.2 = (f32[8,8,128]{2,1,0:T(8,128)S(1)}, f32[8,8,128]{2,1,0:T(8,128)}, u32[]{:S(2)}) copy-start(f32[8,8,128]{2,1,0:T(8,128)} %param.13) | copy-start | bytes 98308
